TPU v7x, 128 devices: a whole 4x4x4 slice. The times are simulated.
128 devices in a mesh: row: 8 (over y, core), col: 16 (over z, x).
Axes of the slice: x: 4, y: 4, z: 4, core: 2. Of those that a mesh axis runs over, the one named last changes fastest.
Arguments:
- blocks: bfloat16 [512, 10, 256, 256], P(('row', 'col')), may hold values from -0.0625 to 0.0625
- block_scales: float32 [512, 10], P(('row', 'col')), may hold values from 0.15 to 0.6
- columns: int32 [512, 10], P(('row', 'col')), may hold values from 0 to 511, as said below
- live: int32 [512], P(('row', 'col')), may hold values from 3 to 10
- onsite: float32 [131072], P(('row', 'col')), may hold values from -1 to 1
- start_vectors: bfloat16 [131072, 128], P(('row', 'col')), may hold values from -6 to 6
Outputs:
- basis: float32 [131072, 128], P(('row', 'col'))
Inputs may be any that keep to these rules, and one draw needn't show every extreme that they name: `columns`: slot 0 of each block row is the row itself; every column lies within 4 block rows of its row, cyclically over 512, and that distance is reached in both directions in every draw.
All inputs are finite; a program needn't handle non-finite values.
Results may differ from a plain program's by a relative error of at most 0.014.
Values may be sent and summed in bfloat16 or wider, within the bound.
No kernel may reach another device: no remote copies, remote signals or barrier semaphores. Data moves between devices by JAX's collectives and lax.ppermute only.
A program may use at most 128 MiB of HBM per device.

v0:
```python
import jax
import jax.numpy as jnp
from jax import lax
from jax.experimental import pallas as pl
from jax.experimental.pallas import tpu as pltpu
from jax.sharding import PartitionSpec as P

DEG = 5
B = 256
K = 128
ROWS = 4
OWN = ROWS * B
REACH = 4
SPAN = 2 * REACH + 1
AXES = ("row", "col")
ALPHA = 2.0 / 1.1
SHIFT = 0.2
F32 = jnp.float32
BF16 = jnp.bfloat16
EDGE = (8, 9, 2, 3)
TO_RIGHT = ((2, 10), (3, 10), (3, 11))
TO_LEFT = ((0, 0), (0, 1), (1, 1))
HANDED = 3 * 2 * B


def rows(i, n=1):
    return pl.ds(i * B, n * B)


def dot(a, b):
    return jnp.dot(a, b, preferred_element_type=F32)


def read_block(ref, i):
    return jnp.concatenate([ref[rows(2 * i), :], ref[rows(2 * i + 1), :]], axis=1)


def flip(block):
    return block.astype(F32).T


def prep_kernel(weight, offset, live, blocks, y0, own, edge, to_right, to_left, buf, acc, sem):
    copies = [pltpu.make_async_copy(blocks.at[a], buf.at[a], sem.at[a]) for a in range(ROWS)]
    for copy in copies:
        copy.start()
    for a in range(ROWS):
        acc[...] = jnp.zeros_like(acc)
        copies[a].wait()

        def add_slot(s, carry, a=a):
            o = offset[a, s]
            acc[o] = acc[o] + weight[a, s] * buf[a, s].astype(F32)
            return carry

        lax.fori_loop(0, live[a], add_slot, 0)
        for o in range(SPAN):
            p = a + o
            value = acc[o].astype(BF16)
            if 4 <= p < 8:
                own[rows(a), rows(p - 4)] = value
            elif p in EDGE:
                edge[rows(a), rows(EDGE.index(p))] = value
            else:
                places, target = (TO_RIGHT, to_right) if p > 8 else (TO_LEFT, to_left)
                i = places.index((a, p))
                target[rows(2 * i), :] = value[:, :K]
                target[rows(2 * i + 1), :] = value[:, K:]
    edge[rows(0), rows(1)] = jnp.zeros((B, B), BF16)
    edge[rows(3), rows(2)] = jnp.zeros((B, B), BF16)
    turned = flip(y0[...]).astype(BF16)
    terms = dot(turned, edge[...]).T.astype(BF16)
    to_right[pl.ds(HANDED, 2 * B), :] = terms[: 2 * B]
    to_left[pl.ds(HANDED, 2 * B), :] = terms[2 * B :]


def first_local_kernel(own, edge, diag, y0, left, right, to_right, to_left, sym, edge_t, base):
    for a in range(ROWS):
        for b in range(a + 1):
            value = own[rows(a), rows(b)].astype(F32) + flip(own[rows(b), rows(a)])
            sym[rows(a), rows(b)] = value.astype(BF16)
            if b < a:
                sym[rows(b), rows(a)] = value.T.astype(BF16)
    for a in range(ROWS):
        for j in range(4):
            edge_t[rows(j), rows(a)] = flip(edge[rows(a), rows(j)]).astype(BF16)
    base[...] = diag[...] * y0[...].astype(F32) + dot(sym[...], y0[...])
    for places, source, halo, first in ((TO_LEFT, to_left, left, 0), (TO_RIGHT, to_right, right, 8)):
        for i, (a, p) in enumerate(places):
            base[rows(a), :] += dot(read_block(source, i), halo[rows(p - first), :])


def send_parts(y, terms, send_right, send_left):
    send_right[pl.ds(0, 2 * B), :] = y[2 * B :]
    send_right[pl.ds(2 * B, 2 * B), :] = terms[: 2 * B]
    send_left[pl.ds(0, 2 * B), :] = y[: 2 * B]
    send_left[pl.ds(2 * B, 2 * B), :] = terms[2 * B :]


def first_post_kernel(base, edge_in, edge_t_in, left, right, got_left, got_right, edge, edge_t, y_out, send_right, send_left):
    edge[...] = edge_in[...]
    edge_t[...] = edge_t_in[...]
    for i, (r, c) in enumerate(TO_LEFT):
        block = read_block(got_right, i).astype(F32)
        edge_t[rows(r), rows(c)] = (edge_t[rows(r), rows(c)].astype(F32) + block).astype(BF16)
        edge[rows(c), rows(r)] = (edge[rows(c), rows(r)].astype(F32) + block.T).astype(BF16)
    for i, (c, p) in enumerate(TO_RIGHT):
        block = read_block(got_left, i).astype(F32)
        r = p - 8
        edge_t[rows(c), rows(r)] = (edge_t[rows(c), rows(r)].astype(F32) + block).astype(BF16)
        edge[rows(r), rows(c)] = (edge[rows(r), rows(c)].astype(F32) + block.T).astype(BF16)
    halo = jnp.concatenate([right[pl.ds(0, 2 * B), :], left[pl.ds(2 * B, 2 * B), :]], axis=0)
    terms = jnp.concatenate([got_left[pl.ds(HANDED, 2 * B), :], got_right[pl.ds(HANDED, 2 * B), :]], axis=0)
    total = base[...] + dot(edge[...], halo) + terms.astype(F32)
    y = (0.5 * total).astype(BF16)
    y_out[...] = y
    send_parts(y, dot(edge_t[...], y).astype(BF16), send_right, send_left)


def received(base, edge, got_left, got_right):
    halo = jnp.concatenate([got_right[pl.ds(0, 2 * B), :], got_left[pl.ds(0, 2 * B), :]], axis=0)
    terms = jnp.concatenate([got_left[pl.ds(2 * B, 2 * B), :], got_right[pl.ds(2 * B, 2 * B), :]], axis=0)
    return (base[...] + dot(edge[...], halo) + terms.astype(F32)).astype(BF16)


def post_kernel(base, edge, edge_t, got_left, got_right, y_out, send_right, send_left):
    y = received(base, edge, got_left, got_right)
    y_out[...] = y
    send_parts(y, dot(edge_t[...], y).astype(BF16), send_right, send_left)


def last_kernel(base, edge, got_left, got_right, y_out, gram):
    y = received(base, edge, got_left, got_right)
    y_out[...] = y
    gram[...] = lax.dot_general(y, y, (((0,), (0,)), ((), ())), preferred_element_type=F32)


def local_kernel(sym, diag, y, older, base):
    base[...] = diag[...] * y[...].astype(F32) - older[...].astype(F32) + dot(sym[...], y[...])


VMEM = pl.BlockSpec(memory_space=pltpu.VMEM)
SMEM = pl.BlockSpec(memory_space=pltpu.SMEM)
ANY = pl.BlockSpec(memory_space=pl.ANY)
LIMIT = 32 * 1024 * 1024


def call(kernel, outs, specs, flops, size, scratch=(), aliases=None):
    return pl.pallas_call(
        kernel,
        out_shape=[jax.ShapeDtypeStruct(*out) for out in outs],
        in_specs=list(specs),
        out_specs=[VMEM] * len(outs),
        scratch_shapes=list(scratch),
        input_output_aliases=aliases or {},
        cost_estimate=pl.CostEstimate(flops=flops, bytes_accessed=size, transcendentals=0),
        compiler_params=pltpu.CompilerParams(vmem_limit_bytes=LIMIT),
    )


def ring(value, step):
    count = lax.axis_size(AXES)
    return lax.ppermute(value, AXES, [(i, (i + step) % count) for i in range(count)])


def group_sum(value, stride, size):
    count = lax.axis_size(AXES)
    parts = [value]
    for step in range(1, size):
        pairs = []
        for i in range(count):
            digit = (i // stride) % size
            pairs.append((i, i + ((digit + step) % size - digit) * stride))
        parts.append(lax.ppermute(value, AXES, pairs))
    return sum(parts[1:], parts[0])


def digits():
    out, stride = [], 1
    for axis, cut in (("col", 4), ("row", 2)):
        left = lax.axis_size(axis)
        while left > 1:
            size = cut if left % cut == 0 else left
            out.append((stride, size))
            stride *= size
            left //= size
            cut = left if axis == "row" else cut
    return out


def local(blocks, block_scales, columns, live, onsite, start_vectors):
    slots = columns.shape[1]
    total = ROWS * lax.axis_size(AXES)
    row_ids = lax.axis_index(AXES) * ROWS + jnp.arange(ROWS, dtype=jnp.int32)
    offset = (columns - row_ids[:, None] + REACH) % total
    weight = block_scales * ALPHA
    diag = (ALPHA * (onsite - SHIFT))[:, None]
    tall = ((OWN, K), BF16)
    tall32 = ((OWN, K), F32)
    square = ((OWN, OWN), BF16)
    handed = ((HANDED + 2 * B, K), BF16)
    product = 2 * OWN * OWN * K

    y0 = start_vectors
    left, right = ring(y0, 1), ring(y0, -1)
    own, edge, to_right, to_left = call(
        prep_kernel,
        [square, square, handed, handed],
        [SMEM, SMEM, SMEM, ANY, VMEM],
        product,
        10_000_000,
        [
            pltpu.VMEM((ROWS, slots, B, B), BF16),
            pltpu.VMEM((SPAN, B, B), F32),
            pltpu.SemaphoreType.DMA((ROWS,)),
        ],
    )(weight, offset, live, blocks, y0)
    got_left, got_right = ring(to_right, 1), ring(to_left, -1)
    sym, edge_t, base = call(first_local_kernel, [square, square, tall32], [VMEM] * 8, product, 10_000_000)(
        own, edge, diag, y0, left, right, to_right, to_left
    )
    edge, edge_t, y, send_right, send_left = call(
        first_post_kernel, [square, square, tall, tall, tall], [VMEM] * 7, 2 * product, 9_000_000, (), {1: 0, 2: 1}
    )(base, edge, edge_t, left, right, got_left, got_right)
    older = y0
    for step in range(1, DEG):
        got_left, got_right = ring(send_right, 1), ring(send_left, -1)
        base = call(local_kernel, [tall32], [VMEM] * 4, product, 3_500_000)(sym, diag, y, older)[0]
        older = y
        if step < DEG - 1:
            y, send_right, send_left = call(post_kernel, [tall, tall, tall], [VMEM] * 5, 2 * product, 6_000_000)(
                base, edge, edge_t, got_left, got_right
            )
        else:
            y, gram = call(last_kernel, [tall, ((K, K), F32)], [VMEM] * 4, product, 4_000_000)(
                base, edge, got_left, got_right
            )
    for stride, size in digits():
        gram = group_sum(gram, stride, size)
    lower = jnp.linalg.cholesky(gram)
    solved = lax.linalg.triangular_solve(lower, y.astype(F32), left_side=False, lower=True, transpose_a=True)
    return solved * jnp.sqrt(F32(total * B))


def solution(mesh):
    return jax.shard_map(
        local,
        mesh=mesh,
        in_specs=(
            P(AXES, None, None, None),
            P(AXES, None),
            P(AXES, None),
            P(AXES),
            P(AXES),
            P(AXES, None),
        ),
        out_specs=P(AXES, None),
        check_vma=False,
    )
```

profile of v0, /device:TPU:0, one launch (start us, length us, event | category | flops | bytes accessed | tf_op | source)
XLA Modules:
  0.0 157.9 jit_solution(1939381450927021279)
XLA Ops:
  0.0 0.7 broadcast_multiply_fusion.weight
  0.7 0.8 add_select_fusion.offset
  1.4 2.5 %copy-done = bf16[4,10,256,256]{3,2,1,0:T(8,128)(2,1)S(1)} copy-done((bf16[4,10,256,256]{3,2,1,0:T(8,128)(2,1)S(1)}, bf16[4,10,256,256]{3,2,1,0:T(8,128)(2,1)}, u32[]{:S(2)}) %copy-start) | copy-done | bytes 5242904
  3.9 0.7 copy-done.3
  4.6 4.5 %shard_map.64 = (bf16[1024,1024]{1,0:T(8,128)(2,1)S(1)}, bf16[1024,1024]{1,0:T(8,128)(2,1)S(1)}, bf16[2048,128]{1,0:T(8,128)(2,1)}, bf16[2048,128]{1,0:T(8,128)(2,1)}) custom-call(f32[4,10]{1,0:T(4,128)S(1)} %broadcast_multiply_fusion.weight, s32[4,10]{1,0:T(4,128)S(1)} %add_select_fusion.offset, s32[4]{0:T(128)S(1)} %copy-done.3, ...), custom_call_target="tpu_custom_call" | custom-call | flops 268435456 | bytes 10000000 | tf_op jit(solution)/shard_map/pallas_call | solution.py:205
  9.1 1.3 copy-done.1
  10.5 1.8 %collective-permute-start.2 = (bf16[2048,128]{1,0:T(8,128)(2,1)}, bf16[2048,128]{1,0:T(8,128)(2,1)}, u32[]{:S(2)}, u32[]{:S(2)}) collective-permute-start(bf16[2048,128]{1,0:T(8,128)(2,1)} %get-tuple-element.30.to_right), channel_id=1, source_target_pairs={{0,1},{1,2},{2,3},{3,4},{4,5},{5,6},{6,7},{7,8},{8,9},{9,10},{10,1... | collective-permute-start | bytes 1572872 | tf_op jit(solution)/shard_map/ppermute | solution.py:162
  12.2 6.7 %collective-permute-start.3 = (bf16[2048,128]{1,0:T(8,128)(2,1)}, bf16[2048,128]{1,0:T(8,128)(2,1)}, u32[]{:S(2)}, u32[]{:S(2)}) collective-permute-start(bf16[2048,128]{1,0:T(8,128)(2,1)} %get-tuple-element.31.to_left), channel_id=1, source_target_pairs={{0,127},{1,0},{2,1},{3,2},{4,3},{5,4},{6,5},{7,6},{8,7},{9,8},{10,... | collective-permute-start | bytes 1572872 | tf_op jit(solution)/shard_map/ppermute | solution.py:162
  18.9 1.5 collective-permute-start.1
  20.4 0.6 collective-permute-start
  20.9 0.2 copy.14.diag
  21.2 13.6 %collective-permute-done.1.right = bf16[1024,128]{1,0:T(8,128)(2,1)S(1)} collective-permute-done((bf16[1024,128]{1,0:T(8,128)(2,1)}, bf16[1024,128]{1,0:T(8,128)(2,1)S(1)}, u32[]{:S(2)}, u32[]{:S(2)}) %collective-permute-start.1) | collective-permute-done | bytes 262176 | tf_op jit(solution)/shard_map/ppermute | solution.py:162
  34.8 1.6 %collective-permute-done.left = bf16[1024,128]{1,0:T(8,128)(2,1)S(1)} collective-permute-done((bf16[1024,128]{1,0:T(8,128)(2,1)}, bf16[1024,128]{1,0:T(8,128)(2,1)S(1)}, u32[]{:S(2)}, u32[]{:S(2)}) %collective-permute-start) | collective-permute-done | bytes 262176 | tf_op jit(solution)/shard_map/ppermute | solution.py:162
  36.5 1.6 %copy-done.2 = bf16[1024,1024]{1,0:T(8,128)(2,1)S(1)} copy-done((bf16[1024,1024]{1,0:T(8,128)(2,1)S(1)}, bf16[1024,1024]{1,0:T(8,128)(2,1)}, u32[]{:S(2)}) %copy-start.2) | copy-done | bytes 2097176
  38.1 2.9 %shard_map.65 = (bf16[1024,1024]{1,0:T(8,128)(2,1)S(1)}, bf16[1024,1024]{1,0:T(8,128)(2,1)S(1)}, f32[1024,128]{1,0:T(8,128)S(1)}) custom-call(bf16[1024,1024]{1,0:T(8,128)(2,1)S(1)} %copy-done.2, bf16[1024,1024]{1,0:T(8,128)(2,1)S(1)} %get-tuple-element.29.edge.edge_in, f32[1024,1]{1,0:T(8,128)S(1)} %copy.14.diag, bf16[1024,128]{1,0:T(8,128)(2,1)} %older.1, ...), custom_call_target="tpu_custom_call" | custom-call | flops 268435456 | bytes 10000000 | tf_op jit(solution)/shard_map/pallas_call | solution.py:218
  41.0 0.0 collective-permute-done.2.got_left
  41.0 3.8 %shard_map.66 = (bf16[1024,1024]{1,0:T(8,128)(2,1)S(1)}, bf16[1024,1024]{1,0:T(8,128)(2,1)S(1)}, bf16[1024,128]{1,0:T(8,128)(2,1)S(1)}, bf16[1024,128]{1,0:T(8,128)(2,1)S(1)}, bf16[1024,128]{1,0:T(8,128)(2,1)S(1)}) custom-call(f32[1024,128]{1,0:T(8,128)S(1)} %get-tuple-element.33.base, ...), custom_call_target="tpu_custom_call", output_to_operand_aliasing={{0}: (1, {}), {1}: (2, {})} | custom-call | flops 536870912 | bytes 9000000 | tf_op jit(solution)/shard_map/pallas_call | solution.py:221
  44.9 0.1 collective-permute-start.4
  45.0 7.2 %collective-permute-start.5 = (bf16[1024,128]{1,0:T(8,128)(2,1)S(1)}, bf16[1024,128]{1,0:T(8,128)(2,1)S(1)}, u32[]{:S(2)}, u32[]{:S(2)}) collective-permute-start(bf16[1024,128]{1,0:T(8,128)(2,1)S(1)} %get-tuple-element.39), channel_id=1, source_target_pairs={{0,127},{1,0},{2,1},{3,2},{4,3},{5,4},{6,5},{7,6},{8,7},{9,8},{10,... | collective-permute-start | bytes 786440 | tf_op jit(solution)/shard_map/ppermute | solution.py:162
  52.1 1.7 %shard_map.67.base = f32[1024,128]{1,0:T(8,128)S(1)} custom-call(bf16[1024,1024]{1,0:T(8,128)(2,1)S(1)} %get-tuple-element.32.sym, f32[1024,1]{1,0:T(8,128)S(1)} %copy.14.diag, bf16[1024,128]{1,0:T(8,128)(2,1)S(1)} %get-tuple-element.35.y.older, bf16[1024,128]{1,0:T(8,128)(2,1)} %older.1), custom_call_target="tpu_custom_call" | custom-call | flops 268435456 | bytes 3500000 | tf_op jit(solution)/shard_map/pallas_call | solution.py:227
  53.8 4.9 %collective-permute-done.4.got_left = bf16[1024,128]{1,0:T(8,128)(2,1)S(1)} collective-permute-done((bf16[1024,128]{1,0:T(8,128)(2,1)S(1)}, bf16[1024,128]{1,0:T(8,128)(2,1)S(1)}, u32[]{:S(2)}, u32[]{:S(2)}) %collective-permute-start.4) | collective-permute-done | bytes 262176 | tf_op jit(solution)/shard_map/ppermute | solution.py:162
  58.7 0.0 collective-permute-done.5.got_right
  58.7 2.2 %shard_map.68 = (bf16[1024,128]{1,0:T(8,128)(2,1)S(1)}, bf16[1024,128]{1,0:T(8,128)(2,1)S(1)}, bf16[1024,128]{1,0:T(8,128)(2,1)S(1)}) custom-call(f32[1024,128]{1,0:T(8,128)S(1)} %shard_map.67.base, bf16[1024,1024]{1,0:T(8,128)(2,1)S(1)} %get-tuple-element.36.edge, bf16[1024,1024]{1,0:T(8,128)(2,1)S(1)} %get-tuple-element.37.edge_t, ...), custom_call_target="tpu_custom_call" | custom-call | flops 536870912 | bytes 6000000 | tf_op jit(solution)/shard_map/pallas_call | solution.py:230
  60.9 0.1 collective-permute-start.6
  61.0 7.2 %collective-permute-start.7 = (bf16[1024,128]{1,0:T(8,128)(2,1)S(1)}, bf16[1024,128]{1,0:T(8,128)(2,1)S(1)}, u32[]{:S(2)}, u32[]{:S(2)}) collective-permute-start(bf16[1024,128]{1,0:T(8,128)(2,1)S(1)} %get-tuple-element.42), channel_id=1, source_target_pairs={{0,127},{1,0},{2,1},{3,2},{4,3},{5,4},{6,5},{7,6},{8,7},{9,8},{10,... | collective-permute-start | bytes 786440 | tf_op jit(solution)/shard_map/ppermute | solution.py:162
  68.2 0.7 shard_map.69.base
  68.9 6.0 %collective-permute-done.6.got_left = bf16[1024,128]{1,0:T(8,128)(2,1)S(1)} collective-permute-done((bf16[1024,128]{1,0:T(8,128)(2,1)S(1)}, bf16[1024,128]{1,0:T(8,128)(2,1)S(1)}, u32[]{:S(2)}, u32[]{:S(2)}) %collective-permute-start.6) | collective-permute-done | bytes 262176 | tf_op jit(solution)/shard_map/ppermute | solution.py:162
  74.9 2.2 %shard_map.70 = (bf16[1024,128]{1,0:T(8,128)(2,1)S(1)}, bf16[1024,128]{1,0:T(8,128)(2,1)S(1)}, bf16[1024,128]{1,0:T(8,128)(2,1)S(1)}) custom-call(f32[1024,128]{1,0:T(8,128)S(1)} %shard_map.69.base, bf16[1024,1024]{1,0:T(8,128)(2,1)S(1)} %get-tuple-element.36.edge, bf16[1024,1024]{1,0:T(8,128)(2,1)S(1)} %get-tuple-element.37.edge_t, ...), custom_call_target="tpu_custom_call" | custom-call | flops 536870912 | bytes 6000000 | tf_op jit(solution)/shard_map/pallas_call | solution.py:230
  77.1 0.1 collective-permute-start.8
  77.2 7.2 %collective-permute-start.9 = (bf16[1024,128]{1,0:T(8,128)(2,1)S(1)}, bf16[1024,128]{1,0:T(8,128)(2,1)S(1)}, u32[]{:S(2)}, u32[]{:S(2)}) collective-permute-start(bf16[1024,128]{1,0:T(8,128)(2,1)S(1)} %get-tuple-element.45), channel_id=1, source_target_pairs={{0,127},{1,0},{2,1},{3,2},{4,3},{5,4},{6,5},{7,6},{8,7},{9,8},{10,... | collective-permute-start | bytes 786440 | tf_op jit(solution)/shard_map/ppermute | solution.py:162
  84.4 0.7 shard_map.71.base
  85.1 5.2 %collective-permute-done.8.got_left = bf16[1024,128]{1,0:T(8,128)(2,1)S(1)} collective-permute-done((bf16[1024,128]{1,0:T(8,128)(2,1)S(1)}, bf16[1024,128]{1,0:T(8,128)(2,1)S(1)}, u32[]{:S(2)}, u32[]{:S(2)}) %collective-permute-start.8) | collective-permute-done | bytes 262176 | tf_op jit(solution)/shard_map/ppermute | solution.py:162
  90.3 2.2 %shard_map.72 = (bf16[1024,128]{1,0:T(8,128)(2,1)S(1)}, bf16[1024,128]{1,0:T(8,128)(2,1)S(1)}, bf16[1024,128]{1,0:T(8,128)(2,1)S(1)}) custom-call(f32[1024,128]{1,0:T(8,128)S(1)} %shard_map.71.base, bf16[1024,1024]{1,0:T(8,128)(2,1)S(1)} %get-tuple-element.36.edge, bf16[1024,1024]{1,0:T(8,128)(2,1)S(1)} %get-tuple-element.37.edge_t, ...), custom_call_target="tpu_custom_call" | custom-call | flops 536870912 | bytes 6000000 | tf_op jit(solution)/shard_map/pallas_call | solution.py:230
  92.5 0.1 collective-permute-start.10
  92.6 7.2 %collective-permute-start.11 = (bf16[1024,128]{1,0:T(8,128)(2,1)S(1)}, bf16[1024,128]{1,0:T(8,128)(2,1)S(1)}, u32[]{:S(2)}, u32[]{:S(2)}) collective-permute-start(bf16[1024,128]{1,0:T(8,128)(2,1)S(1)} %get-tuple-element.48), channel_id=1, source_target_pairs={{0,127},{1,0},{2,1},{3,2},{4,3},{5,4},{6,5},{7,6},{8,7},{9,8},{10,... | collective-permute-start | bytes 786440 | tf_op jit(solution)/shard_map/ppermute | solution.py:162
  99.8 0.7 shard_map.73.base
  100.5 4.3 %collective-permute-done.10.got_left = bf16[1024,128]{1,0:T(8,128)(2,1)S(1)} collective-permute-done((bf16[1024,128]{1,0:T(8,128)(2,1)S(1)}, bf16[1024,128]{1,0:T(8,128)(2,1)S(1)}, u32[]{:S(2)}, u32[]{:S(2)}) %collective-permute-start.10) | collective-permute-done | bytes 262176 | tf_op jit(solution)/shard_map/ppermute | solution.py:162
  104.8 0.9 shard_map.74
  105.7 0.1 copy.20
  105.8 0.1 collective-permute-start.14
  105.9 0.1 collective-permute-start.13
  106.0 1.9 %collective-permute-start.12 = (f32[128,128]{0,1:T(8,128)S(1)}, f32[128,128]{0,1:T(8,128)S(1)}, u32[]{:S(2)}, u32[]{:S(2)}) collective-permute-start(f32[128,128]{0,1:T(8,128)S(1)} %copy.20), channel_id=1, source_target_pairs={{0,1},{1,2},{2,3},{3,0},{4,5},{5,6},{6,7},{7,4},{8,9},{9,10},{10,1... | collective-permute-start | bytes 196616 | tf_op jit(solution)/shard_map/ppermute | solution.py:173
  107.9 2.2 %collective-permute-done.14 = f32[128,128]{0,1:T(8,128)S(1)} collective-permute-done((f32[128,128]{0,1:T(8,128)S(1)}, f32[128,128]{0,1:T(8,128)S(1)}, u32[]{:S(2)}, u32[]{:S(2)}) %collective-permute-start.14) | collective-permute-done | bytes 65568 | tf_op jit(solution)/shard_map/ppermute | solution.py:173
  110.1 1.6 %collective-permute-done.13 = f32[128,128]{0,1:T(8,128)S(1)} collective-permute-done((f32[128,128]{0,1:T(8,128)S(1)}, f32[128,128]{0,1:T(8,128)S(1)}, u32[]{:S(2)}, u32[]{:S(2)}) %collective-permute-start.13) | collective-permute-done | bytes 65568 | tf_op jit(solution)/shard_map/ppermute | solution.py:173
  111.7 1.1 collective-permute-done.12
  112.8 0.1 collective-permute-start.17
  112.9 0.1 collective-permute-start.16
  113.0 1.9 %collective-permute-start.15 = (f32[128,128]{0,1:T(8,128)S(1)}, f32[128,128]{0,1:T(8,128)S(1)}, u32[]{:S(2)}, u32[]{:S(2)}) collective-permute-start(f32[128,128]{0,1:T(8,128)S(1)} %add_add_fusion.2), channel_id=1, source_target_pairs={{0,4},{1,5},{2,6},{3,7},{4,8},{5,9},{6,10},{7,11},{8,12},{9,13},{1... | collective-permute-start | bytes 196616 | tf_op jit(solution)/shard_map/ppermute | solution.py:173
  114.9 2.2 %collective-permute-done.17 = f32[128,128]{0,1:T(8,128)S(1)} collective-permute-done((f32[128,128]{0,1:T(8,128)S(1)}, f32[128,128]{0,1:T(8,128)S(1)}, u32[]{:S(2)}, u32[]{:S(2)}) %collective-permute-start.17) | collective-permute-done | bytes 65568 | tf_op jit(solution)/shard_map/ppermute | solution.py:173
  117.1 1.6 %collective-permute-done.16 = f32[128,128]{0,1:T(8,128)S(1)} collective-permute-done((f32[128,128]{0,1:T(8,128)S(1)}, f32[128,128]{0,1:T(8,128)S(1)}, u32[]{:S(2)}, u32[]{:S(2)}) %collective-permute-start.16) | collective-permute-done | bytes 65568 | tf_op jit(solution)/shard_map/ppermute | solution.py:173
  118.7 1.1 collective-permute-done.15
  119.8 0.1 collective-permute-start.18
  119.9 1.2 collective-permute-done.18
  121.2 6.1 %collective-permute-start.21 = (f32[128,128]{0,1:T(8,128)S(1)}, f32[128,128]{0,1:T(8,128)S(1)}, u32[]{:S(2)}, u32[]{:S(2)}) collective-permute-start(f32[128,128]{0,1:T(8,128)S(1)} %add.79), channel_id=1, source_target_pairs={{0,96},{1,97},{2,98},{3,99},{4,100},{5,101},{6,102},{7,103},{8,104... | collective-permute-start | bytes 196616 | tf_op jit(solution)/shard_map/ppermute | solution.py:173
  127.3 0.9 collective-permute-start.19
  128.2 2.2 %collective-permute-done.21 = f32[128,128]{0,1:T(8,128)S(1)} collective-permute-done((f32[128,128]{0,1:T(8,128)S(1)}, f32[128,128]{0,1:T(8,128)S(1)}, u32[]{:S(2)}, u32[]{:S(2)}) %collective-permute-start.21) | collective-permute-done | bytes 65568 | tf_op jit(solution)/shard_map/ppermute | solution.py:173
  130.4 3.0 %collective-permute-done.20 = f32[128,128]{0,1:T(8,128)S(1)} collective-permute-done((f32[128,128]{0,1:T(8,128)S(1)}, f32[128,128]{0,1:T(8,128)S(1)}, u32[]{:S(2)}, u32[]{:S(2)}) %collective-permute-start.20) | collective-permute-done | bytes 65568 | tf_op jit(solution)/shard_map/ppermute | solution.py:173
  133.4 0.4 collective-permute-done.19
  133.8 0.1 copy.23
  133.9 11.7 %cholesky.16 = f32[128,128]{1,0:T(8,128)S(1)} custom-call(f32[128,128]{1,0:T(8,128)S(1)} %fusion.2), custom_call_target="Cholesky" | custom-call | tf_op jit(solution)/shard_map/jit(cholesky)/cholesky | solution.py:239
  145.6 0.6 compare_reduce_fusion
  146.3 0.7 fusion
  146.9 9.8 %custom-call.6 = f32[1,128,128]{1,2,0:T(8,128)S(1)} custom-call(f32[1,128,128]{2,1,0:T(8,128)S(1)} %fusion), custom_call_target="InvertDiagBlocksLowerTriangular" | custom-call | tf_op jit(solution)/shard_map/triangular_solve | solution.py:240
  156.8 1.2 convolution_multiply_fusion
  (19 shorter events, 0.1 us)
Async XLA Ops:
  1.4 2.5 %copy-start = (bf16[4,10,256,256]{3,2,1,0:T(8,128)(2,1)S(1)}, bf16[4,10,256,256]{3,2,1,0:T(8,128)(2,1)}, u32[]{:S(2)}) copy-start(bf16[4,10,256,256]{3,2,1,0:T(8,128)(2,1)} %blocks.1) | copy-start | bytes 15728644
  3.9 0.7 copy-start.3
  4.6 16.4 %copy-start.4 = (f32[1024]{0:T(1024)S(1)}, f32[1024]{0:T(1024)}, u32[]{:S(2)}) copy-start(f32[1024]{0:T(1024)} %param.10) | copy-start | bytes 12292
  9.1 1.3 copy-start.1
  10.5 30.5 %collective-permute-start.2 = (bf16[2048,128]{1,0:T(8,128)(2,1)}, bf16[2048,128]{1,0:T(8,128)(2,1)}, u32[]{:S(2)}, u32[]{:S(2)}) collective-permute-start(bf16[2048,128]{1,0:T(8,128)(2,1)} %get-tuple-element.30.to_right), channel_id=1, source_target_pairs={{0,1},{1,2},{2,3},{3,4},{4,5},{5,6},{6,7},{7,8},{8,9},{9,10},{10,1... | collective-permute-start | bytes 1572872 | tf_op jit(solution)/shard_map/ppermute | solution.py:162
  12.2 28.8 %collective-permute-start.3 = (bf16[2048,128]{1,0:T(8,128)(2,1)}, bf16[2048,128]{1,0:T(8,128)(2,1)}, u32[]{:S(2)}, u32[]{:S(2)}) collective-permute-start(bf16[2048,128]{1,0:T(8,128)(2,1)} %get-tuple-element.31.to_left), channel_id=1, source_target_pairs={{0,127},{1,0},{2,1},{3,2},{4,3},{5,4},{6,5},{7,6},{8,7},{9,8},{10,... | collective-permute-start | bytes 1572872 | tf_op jit(solution)/shard_map/ppermute | solution.py:162
  18.9 15.9 %collective-permute-start.1 = (bf16[1024,128]{1,0:T(8,128)(2,1)}, bf16[1024,128]{1,0:T(8,128)(2,1)S(1)}, u32[]{:S(2)}, u32[]{:S(2)}) collective-permute-start(bf16[1024,128]{1,0:T(8,128)(2,1)} %older.1), channel_id=1, source_target_pairs={{0,127},{1,0},{2,1},{3,2},{4,3},{5,4},{6,5},{7,6},{8,7},{9,8},{10,... | collective-permute-start | bytes 786440 | tf_op jit(solution)/shard_map/ppermute | solution.py:162
  20.4 16.1 %collective-permute-start = (bf16[1024,128]{1,0:T(8,128)(2,1)}, bf16[1024,128]{1,0:T(8,128)(2,1)S(1)}, u32[]{:S(2)}, u32[]{:S(2)}) collective-permute-start(bf16[1024,128]{1,0:T(8,128)(2,1)} %older.1), channel_id=1, source_target_pairs={{0,1},{1,2},{2,3},{3,4},{4,5},{5,6},{6,7},{7,8},{8,9},{9,10},{10,1... | collective-permute-start | bytes 786440 | tf_op jit(solution)/shard_map/ppermute | solution.py:162
  36.5 1.6 %copy-start.2 = (bf16[1024,1024]{1,0:T(8,128)(2,1)S(1)}, bf16[1024,1024]{1,0:T(8,128)(2,1)}, u32[]{:S(2)}) copy-start(bf16[1024,1024]{1,0:T(8,128)(2,1)} %copy-done.1) | copy-start | bytes 6291460
  44.9 13.8 %collective-permute-start.4 = (bf16[1024,128]{1,0:T(8,128)(2,1)S(1)}, bf16[1024,128]{1,0:T(8,128)(2,1)S(1)}, u32[]{:S(2)}, u32[]{:S(2)}) collective-permute-start(bf16[1024,128]{1,0:T(8,128)(2,1)S(1)} %get-tuple-element.38), channel_id=1, source_target_pairs={{0,1},{1,2},{2,3},{3,4},{4,5},{5,6},{6,7},{7,8},{8,9},{9,10},{10,1... | collective-permute-start | bytes 786440 | tf_op jit(solution)/shard_map/ppermute | solution.py:162
  45.0 13.7 %collective-permute-start.5 = (bf16[1024,128]{1,0:T(8,128)(2,1)S(1)}, bf16[1024,128]{1,0:T(8,128)(2,1)S(1)}, u32[]{:S(2)}, u32[]{:S(2)}) collective-permute-start(bf16[1024,128]{1,0:T(8,128)(2,1)S(1)} %get-tuple-element.39), channel_id=1, source_target_pairs={{0,127},{1,0},{2,1},{3,2},{4,3},{5,4},{6,5},{7,6},{8,7},{9,8},{10,... | collective-permute-start | bytes 786440 | tf_op jit(solution)/shard_map/ppermute | solution.py:162
  60.9 13.9 %collective-permute-start.6 = (bf16[1024,128]{1,0:T(8,128)(2,1)S(1)}, bf16[1024,128]{1,0:T(8,128)(2,1)S(1)}, u32[]{:S(2)}, u32[]{:S(2)}) collective-permute-start(bf16[1024,128]{1,0:T(8,128)(2,1)S(1)} %get-tuple-element.41), channel_id=1, source_target_pairs={{0,1},{1,2},{2,3},{3,4},{4,5},{5,6},{6,7},{7,8},{8,9},{9,10},{10,1... | collective-permute-start | bytes 786440 | tf_op jit(solution)/shard_map/ppermute | solution.py:162
  61.0 13.8 %collective-permute-start.7 = (bf16[1024,128]{1,0:T(8,128)(2,1)S(1)}, bf16[1024,128]{1,0:T(8,128)(2,1)S(1)}, u32[]{:S(2)}, u32[]{:S(2)}) collective-permute-start(bf16[1024,128]{1,0:T(8,128)(2,1)S(1)} %get-tuple-element.42), channel_id=1, source_target_pairs={{0,127},{1,0},{2,1},{3,2},{4,3},{5,4},{6,5},{7,6},{8,7},{9,8},{10,... | collective-permute-start | bytes 786440 | tf_op jit(solution)/shard_map/ppermute | solution.py:162
  77.1 13.2 %collective-permute-start.8 = (bf16[1024,128]{1,0:T(8,128)(2,1)S(1)}, bf16[1024,128]{1,0:T(8,128)(2,1)S(1)}, u32[]{:S(2)}, u32[]{:S(2)}) collective-permute-start(bf16[1024,128]{1,0:T(8,128)(2,1)S(1)} %get-tuple-element.44), channel_id=1, source_target_pairs={{0,1},{1,2},{2,3},{3,4},{4,5},{5,6},{6,7},{7,8},{8,9},{9,10},{10,1... | collective-permute-start | bytes 786440 | tf_op jit(solution)/shard_map/ppermute | solution.py:162
  77.2 13.1 %collective-permute-start.9 = (bf16[1024,128]{1,0:T(8,128)(2,1)S(1)}, bf16[1024,128]{1,0:T(8,128)(2,1)S(1)}, u32[]{:S(2)}, u32[]{:S(2)}) collective-permute-start(bf16[1024,128]{1,0:T(8,128)(2,1)S(1)} %get-tuple-element.45), channel_id=1, source_target_pairs={{0,127},{1,0},{2,1},{3,2},{4,3},{5,4},{6,5},{7,6},{8,7},{9,8},{10,... | collective-permute-start | bytes 786440 | tf_op jit(solution)/shard_map/ppermute | solution.py:162
  92.5 12.2 %collective-permute-start.10 = (bf16[1024,128]{1,0:T(8,128)(2,1)S(1)}, bf16[1024,128]{1,0:T(8,128)(2,1)S(1)}, u32[]{:S(2)}, u32[]{:S(2)}) collective-permute-start(bf16[1024,128]{1,0:T(8,128)(2,1)S(1)} %get-tuple-element.47), channel_id=1, source_target_pairs={{0,1},{1,2},{2,3},{3,4},{4,5},{5,6},{6,7},{7,8},{8,9},{9,10},{10,1... | collective-permute-start | bytes 786440 | tf_op jit(solution)/shard_map/ppermute | solution.py:162
  92.6 12.2 %collective-permute-start.11 = (bf16[1024,128]{1,0:T(8,128)(2,1)S(1)}, bf16[1024,128]{1,0:T(8,128)(2,1)S(1)}, u32[]{:S(2)}, u32[]{:S(2)}) collective-permute-start(bf16[1024,128]{1,0:T(8,128)(2,1)S(1)} %get-tuple-element.48), channel_id=1, source_target_pairs={{0,127},{1,0},{2,1},{3,2},{4,3},{5,4},{6,5},{7,6},{8,7},{9,8},{10,... | collective-permute-start | bytes 786440 | tf_op jit(solution)/shard_map/ppermute | solution.py:162
  105.8 4.3 %collective-permute-start.14 = (f32[128,128]{0,1:T(8,128)S(1)}, f32[128,128]{0,1:T(8,128)S(1)}, u32[]{:S(2)}, u32[]{:S(2)}) collective-permute-start(f32[128,128]{0,1:T(8,128)S(1)} %copy.20), channel_id=1, source_target_pairs={{0,3},{1,0},{2,1},{3,2},{4,7},{5,4},{6,5},{7,6},{8,11},{9,8},{10,9... | collective-permute-start | bytes 196616 | tf_op jit(solution)/shard_map/ppermute | solution.py:173
  105.9 5.8 %collective-permute-start.13 = (f32[128,128]{0,1:T(8,128)S(1)}, f32[128,128]{0,1:T(8,128)S(1)}, u32[]{:S(2)}, u32[]{:S(2)}) collective-permute-start(f32[128,128]{0,1:T(8,128)S(1)} %copy.20), channel_id=1, source_target_pairs={{0,2},{1,3},{2,0},{3,1},{4,6},{5,7},{6,4},{7,5},{8,10},{9,11},{10,... | collective-permute-start | bytes 196616 | tf_op jit(solution)/shard_map/ppermute | solution.py:173
  106.0 6.8 %collective-permute-start.12 = (f32[128,128]{0,1:T(8,128)S(1)}, f32[128,128]{0,1:T(8,128)S(1)}, u32[]{:S(2)}, u32[]{:S(2)}) collective-permute-start(f32[128,128]{0,1:T(8,128)S(1)} %copy.20), channel_id=1, source_target_pairs={{0,1},{1,2},{2,3},{3,0},{4,5},{5,6},{6,7},{7,4},{8,9},{9,10},{10,1... | collective-permute-start | bytes 196616 | tf_op jit(solution)/shard_map/ppermute | solution.py:173
  112.8 4.3 %collective-permute-start.17 = (f32[128,128]{0,1:T(8,128)S(1)}, f32[128,128]{0,1:T(8,128)S(1)}, u32[]{:S(2)}, u32[]{:S(2)}) collective-permute-start(f32[128,128]{0,1:T(8,128)S(1)} %add_add_fusion.2), channel_id=1, source_target_pairs={{0,12},{1,13},{2,14},{3,15},{4,0},{5,1},{6,2},{7,3},{8,4},{9,5},{1... | collective-permute-start | bytes 196616 | tf_op jit(solution)/shard_map/ppermute | solution.py:173
  112.9 5.8 %collective-permute-start.16 = (f32[128,128]{0,1:T(8,128)S(1)}, f32[128,128]{0,1:T(8,128)S(1)}, u32[]{:S(2)}, u32[]{:S(2)}) collective-permute-start(f32[128,128]{0,1:T(8,128)S(1)} %add_add_fusion.2), channel_id=1, source_target_pairs={{0,8},{1,9},{2,10},{3,11},{4,12},{5,13},{6,14},{7,15},{8,0},{9,1},... | collective-permute-start | bytes 196616 | tf_op jit(solution)/shard_map/ppermute | solution.py:173
  113.0 6.8 %collective-permute-start.15 = (f32[128,128]{0,1:T(8,128)S(1)}, f32[128,128]{0,1:T(8,128)S(1)}, u32[]{:S(2)}, u32[]{:S(2)}) collective-permute-start(f32[128,128]{0,1:T(8,128)S(1)} %add_add_fusion.2), channel_id=1, source_target_pairs={{0,4},{1,5},{2,6},{3,7},{4,8},{5,9},{6,10},{7,11},{8,12},{9,13},{1... | collective-permute-start | bytes 196616 | tf_op jit(solution)/shard_map/ppermute | solution.py:173
  119.8 1.3 collective-permute-start.18
  121.2 9.2 %collective-permute-start.21 = (f32[128,128]{0,1:T(8,128)S(1)}, f32[128,128]{0,1:T(8,128)S(1)}, u32[]{:S(2)}, u32[]{:S(2)}) collective-permute-start(f32[128,128]{0,1:T(8,128)S(1)} %add.79), channel_id=1, source_target_pairs={{0,96},{1,97},{2,98},{3,99},{4,100},{5,101},{6,102},{7,103},{8,104... | collective-permute-start | bytes 196616 | tf_op jit(solution)/shard_map/ppermute | solution.py:173
  127.3 6.1 %collective-permute-start.20 = (f32[128,128]{0,1:T(8,128)S(1)}, f32[128,128]{0,1:T(8,128)S(1)}, u32[]{:S(2)}, u32[]{:S(2)}) collective-permute-start(f32[128,128]{0,1:T(8,128)S(1)} %add.79), channel_id=1, source_target_pairs={{0,64},{1,65},{2,66},{3,67},{4,68},{5,69},{6,70},{7,71},{8,72},{9,... | collective-permute-start | bytes 196616 | tf_op jit(solution)/shard_map/ppermute | solution.py:173
  127.3 6.5 %collective-permute-start.19 = (f32[128,128]{0,1:T(8,128)S(1)}, f32[128,128]{0,1:T(8,128)S(1)}, u32[]{:S(2)}, u32[]{:S(2)}) collective-permute-start(f32[128,128]{0,1:T(8,128)S(1)} %add.79), channel_id=1, source_target_pairs={{0,32},{1,33},{2,34},{3,35},{4,36},{5,37},{6,38},{7,39},{8,40},{9,... | collective-permute-start | bytes 196616 | tf_op jit(solution)/shard_map/ppermute | solution.py:173
where the time goes:
time: 158 us
  waiting for transfers between devices  52.3 us (33%)
  starting transfers between devices  50.7 us (32%)
  other arithmetic  24.4 us (15%)
  Pallas kernels  22.7 us (14%)
  local copies, waits for them, and re-layouts  6.47 us (4%)
    ppermute x12, starting transfers between devices, ring(): lax.ppermute(value, AXES, [(i, (i + step) % count) for i in range(count)])  39.5 us
    ppermute x12, waiting for transfers between devices, ring(): lax.ppermute(value, AXES, [(i, (i + step) % count) for i in range(count)])  35.7 us
    ppermute x10, waiting for transfers between devices, group_sum(): parts.append(lax.ppermute(value, AXES, pairs))  16.6 us
    another operation x3, other arithmetic, local(): lower = jnp.linalg.cholesky(gram)  12.4 us
    ppermute x10, starting transfers between devices, group_sum(): parts.append(lax.ppermute(value, AXES, pairs))  11.3 us
    another operation x2, other arithmetic, local(): lax.linalg.triangular_solve(lower, y.astype(F32), left_side=False, lower=...  10.5 us
    pallas_call x3, Pallas kernels, local(): call(post_kernel, [tall, tall, tall], [VMEM] * 5, 2 * product, 6000000)  6.7 us
    unnamed x10, local copies, waits for them, and re-layouts  6.07 us
  transfers between devices with their start and end apart: 22, of which 16 were waited for; matrix products, arithmetic and copies ran while one was open for 0% of the time, Pallas kernels for 4%

commit v1 on v0

--- a/solution.py
+++ b/solution.py
@@ -1,5 +1,8 @@
+import functools
+
 import jax
 import jax.numpy as jnp
+import numpy as np
 from jax import lax
 from jax.experimental import pallas as pl
 from jax.experimental.pallas import tpu as pltpu
@@ -21,6 +24,7 @@
 TO_RIGHT = ((2, 10), (3, 10), (3, 11))
 TO_LEFT = ((0, 0), (0, 1), (1, 1))
 HANDED = 3 * 2 * B
+T = 8
 
 
 def rows(i, n=1):
@@ -136,6 +140,59 @@
 
 def local_kernel(sym, diag, y, older, base):
     base[...] = diag[...] * y[...].astype(F32) - older[...].astype(F32) + dot(sym[...], y[...])
+
+
+def lane_fill(x, c):
+    return jnp.take_along_axis(x, jnp.full((T, K), c, jnp.int32), axis=1)
+
+
+def row_fill(x, j):
+    return jnp.take_along_axis(x, jnp.full((T, K), j, jnp.int32), axis=0)
+
+
+def inverse_factor(gram, inverse):
+    count = K // T
+    lane = lax.broadcasted_iota(jnp.int32, (T, K), 1)
+    sub = lax.broadcasted_iota(jnp.int32, (T, K), 0)
+    tiles = [gram[pl.ds(T * t, T), :] for t in range(count)]
+    for k in range(count):
+        first = T * k
+        inside = (lane >= first) & (lane < first + T)
+        spread = [lane_fill(tiles[k], first + c) for c in range(T)]
+        rest = jnp.where(inside, 0.0, tiles[k])
+        steps = []
+        scale = jnp.zeros((T, K), F32)
+        for j in range(T):
+            pivot = row_fill(spread[j], j)
+            inv = 1.0 / pivot
+            ratios = {c: row_fill(spread[c], j) * inv for c in range(j + 1, T)}
+            row = jnp.where(lane == first + j, 1.0, row_fill(rest, j)) * inv
+            steps.append((ratios, row))
+            rest = rest - jnp.where(sub > j, spread[j], 0.0) * row
+            for c in range(j + 1, T):
+                spread[c] = spread[c] - spread[j] * ratios[c]
+            scale = jnp.where(sub == j, lax.rsqrt(pivot), scale)
+        unit = jnp.where(lane < first + sub, rest, jnp.where(lane == first + sub, 1.0, 0.0))
+        inverse[pl.ds(first, T), :] = unit * scale
+        for t in range(k + 1, count):
+            factors = [lane_fill(tiles[t], first + c) for c in range(T)]
+            value = jnp.where(inside, 0.0, tiles[t])
+            for j, (ratios, row) in enumerate(steps):
+                value = value - factors[j] * row
+                for c in range(j + 1, T):
+                    factors[c] = factors[c] - factors[j] * ratios[c]
+            tiles[t] = value
+
+
+def finish_kernel(scale, gram, y, basis, inverse):
+    inverse_factor(gram, inverse)
+    value = inverse[...] * scale
+    high = value.astype(BF16)
+    low = (value - high.astype(F32)).astype(BF16)
+    dims = (((1,), (1,)), ((), ()))
+    basis[...] = lax.dot_general(y[...], high, dims, preferred_element_type=F32) + lax.dot_general(
+        y[...], low, dims, preferred_element_type=F32
+    )
 
 
 VMEM = pl.BlockSpec(memory_space=pltpu.VMEM)
@@ -236,9 +293,10 @@
             )
     for stride, size in digits():
         gram = group_sum(gram, stride, size)
-    lower = jnp.linalg.cholesky(gram)
-    solved = lax.linalg.triangular_solve(lower, y.astype(F32), left_side=False, lower=True, transpose_a=True)
-    return solved * jnp.sqrt(F32(total * B))
+    scale = float(np.sqrt(total * B))
+    return call(
+        functools.partial(finish_kernel, scale), [tall32], [VMEM] * 2, 2 * product, 1_000_000, [pltpu.VMEM((K, K), F32)]
+    )(gram, y)[0]
 
 
 def solution(mesh):

time: 158 us -> 138 us (0.87)
  other arithmetic: 24.4 us -> 1.51 us
  Pallas kernels: 22.7 us -> 27.1 us
    another operation x5 -> x0, other arithmetic: 22.9 us -> none  [the longest x3 12.4 us: local(): lower = jnp.linalg.cholesky(gram)]
    pallas_call x0 -> x1, Pallas kernels: none -> 4.27 us  [local(): call(functools.partial(finish_kernel, scale), [tall32], [VMEM] * 2, 2 * p...]
  transfers between devices with their start and end apart: 22 -> 22, of which waited for: 16 -> 16; matrix products, arithmetic and copies ran while one was open for 0% -> 0% of each run, Pallas kernels for 4% -> 5%
where the time goes in v1:
time: 138 us
  waiting for transfers between devices  52.2 us (38%)
  starting transfers between devices  50.9 us (37%)
  Pallas kernels  27.1 us (20%)
  local copies, waits for them, and re-layouts  6.31 us (5%)
  other arithmetic  1.51 us (1%)
    ppermute x12, starting transfers between devices, ring(): lax.ppermute(value, AXES, [(i, (i + step) % count) for i in range(count)])  39.3 us
    ppermute x12, waiting for transfers between devices, ring(): lax.ppermute(value, AXES, [(i, (i + step) % count) for i in range(count)])  35.6 us
    ppermute x10, waiting for transfers between devices, group_sum(): parts.append(lax.ppermute(value, AXES, pairs))  16.6 us
    ppermute x10, starting transfers between devices, group_sum(): parts.append(lax.ppermute(value, AXES, pairs))  11.6 us
    pallas_call x3, Pallas kernels, local(): call(post_kernel, [tall, tall, tall], [VMEM] * 5, 2 * product, 6000000)  6.7 us
    unnamed x10, local copies, waits for them, and re-layouts  6.08 us
    pallas_call x1, Pallas kernels, local(): call(prep_kernel, [square, square, handed, handed], [SMEM, SMEM, SMEM, AN...  4.66 us
    pallas_call x1, Pallas kernels, local(): call(functools.partial(finish_kernel, scale), [tall32], [VMEM] * 2, 2 * p...  4.27 us
  transfers between devices with their start and end apart: 22, of which 16 were waited for; matrix products, arithmetic and copies ran while one was open for 0% of the time, Pallas kernels for 5%

profile of v1, /device:TPU:0, one launch (start us, length us, event | category | flops | bytes accessed | tf_op | source)
XLA Modules:
  0.0 138.2 jit_solution(5561074922031838802)
XLA Ops:
  0.0 0.7 broadcast_multiply_fusion.weight
  0.7 0.8 add_select_fusion.offset
  1.4 2.5 %copy-done = bf16[4,10,256,256]{3,2,1,0:T(8,128)(2,1)S(1)} copy-done((bf16[4,10,256,256]{3,2,1,0:T(8,128)(2,1)S(1)}, bf16[4,10,256,256]{3,2,1,0:T(8,128)(2,1)}, u32[]{:S(2)}) %copy-start) | copy-done | bytes 5242904
  3.9 0.7 copy-done.3
  4.6 4.7 %shard_map.64 = (bf16[1024,1024]{1,0:T(8,128)(2,1)S(1)}, bf16[1024,1024]{1,0:T(8,128)(2,1)S(1)}, bf16[2048,128]{1,0:T(8,128)(2,1)}, bf16[2048,128]{1,0:T(8,128)(2,1)}) custom-call(f32[4,10]{1,0:T(4,128)S(1)} %broadcast_multiply_fusion.weight, s32[4,10]{1,0:T(4,128)S(1)} %add_select_fusion.offset, s32[4]{0:T(128)S(1)} %copy-done.3, ...), custom_call_target="tpu_custom_call" | custom-call | flops 268435456 | bytes 10000000 | tf_op jit(solution)/shard_map/pallas_call | solution.py:262
  9.3 0.0 copy-start.1
  9.3 1.3 copy-done.1
  10.6 1.8 %collective-permute-start.2 = (bf16[2048,128]{1,0:T(8,128)(2,1)}, bf16[2048,128]{1,0:T(8,128)(2,1)}, u32[]{:S(2)}, u32[]{:S(2)}) collective-permute-start(bf16[2048,128]{1,0:T(8,128)(2,1)} %get-tuple-element.30.to_right), channel_id=1, source_target_pairs={{0,1},{1,2},{2,3},{3,4},{4,5},{5,6},{6,7},{7,8},{8,9},{9,10},{10,1... | collective-permute-start | bytes 1572872 | tf_op jit(solution)/shard_map/ppermute | solution.py:219
  12.4 6.5 %collective-permute-start.3 = (bf16[2048,128]{1,0:T(8,128)(2,1)}, bf16[2048,128]{1,0:T(8,128)(2,1)}, u32[]{:S(2)}, u32[]{:S(2)}) collective-permute-start(bf16[2048,128]{1,0:T(8,128)(2,1)} %get-tuple-element.31.to_left), channel_id=1, source_target_pairs={{0,127},{1,0},{2,1},{3,2},{4,3},{5,4},{6,5},{7,6},{8,7},{9,8},{10,... | collective-permute-start | bytes 1572872 | tf_op jit(solution)/shard_map/ppermute | solution.py:219
  18.9 1.5 %collective-permute-start.1 = (bf16[1024,128]{1,0:T(8,128)(2,1)}, bf16[1024,128]{1,0:T(8,128)(2,1)S(1)}, u32[]{:S(2)}, u32[]{:S(2)}) collective-permute-start(bf16[1024,128]{1,0:T(8,128)(2,1)} %older.1), channel_id=1, source_target_pairs={{0,127},{1,0},{2,1},{3,2},{4,3},{5,4},{6,5},{7,6},{8,7},{9,8},{10,... | collective-permute-start | bytes 786440 | tf_op jit(solution)/shard_map/ppermute | solution.py:219
  20.4 0.6 collective-permute-start
  21.0 0.2 copy.9.diag
  21.2 13.6 %collective-permute-done.1.right = bf16[1024,128]{1,0:T(8,128)(2,1)S(1)} collective-permute-done((bf16[1024,128]{1,0:T(8,128)(2,1)}, bf16[1024,128]{1,0:T(8,128)(2,1)S(1)}, u32[]{:S(2)}, u32[]{:S(2)}) %collective-permute-start.1) | collective-permute-done | bytes 262176 | tf_op jit(solution)/shard_map/ppermute | solution.py:219
  34.8 1.9 %collective-permute-done.left = bf16[1024,128]{1,0:T(8,128)(2,1)S(1)} collective-permute-done((bf16[1024,128]{1,0:T(8,128)(2,1)}, bf16[1024,128]{1,0:T(8,128)(2,1)S(1)}, u32[]{:S(2)}, u32[]{:S(2)}) %collective-permute-start) | collective-permute-done | bytes 262176 | tf_op jit(solution)/shard_map/ppermute | solution.py:219
  36.7 1.6 %copy-done.2 = bf16[1024,1024]{1,0:T(8,128)(2,1)S(1)} copy-done((bf16[1024,1024]{1,0:T(8,128)(2,1)S(1)}, bf16[1024,1024]{1,0:T(8,128)(2,1)}, u32[]{:S(2)}) %copy-start.2) | copy-done | bytes 2097176
  38.2 2.9 %shard_map.65 = (bf16[1024,1024]{1,0:T(8,128)(2,1)S(1)}, bf16[1024,1024]{1,0:T(8,128)(2,1)S(1)}, f32[1024,128]{1,0:T(8,128)S(1)}) custom-call(bf16[1024,1024]{1,0:T(8,128)(2,1)S(1)} %copy-done.2, bf16[1024,1024]{1,0:T(8,128)(2,1)S(1)} %get-tuple-element.29.edge.edge_in, f32[1024,1]{1,0:T(8,128)S(1)} %copy.9.diag, bf16[1024,128]{1,0:T(8,128)(2,1)} %older.1, ...), custom_call_target="tpu_custom_call" | custom-call | flops 268435456 | bytes 10000000 | tf_op jit(solution)/shard_map/pallas_call | solution.py:275
  41.2 0.0 collective-permute-done.2.got_left
  41.2 0.0 collective-permute-done.3.got_right
  41.2 3.8 %shard_map.66 = (bf16[1024,1024]{1,0:T(8,128)(2,1)S(1)}, bf16[1024,1024]{1,0:T(8,128)(2,1)S(1)}, bf16[1024,128]{1,0:T(8,128)(2,1)S(1)}, bf16[1024,128]{1,0:T(8,128)(2,1)S(1)}, bf16[1024,128]{1,0:T(8,128)(2,1)S(1)}) custom-call(f32[1024,128]{1,0:T(8,128)S(1)} %get-tuple-element.33.base, ...), custom_call_target="tpu_custom_call", output_to_operand_aliasing={{0}: (1, {}), {1}: (2, {})} | custom-call | flops 536870912 | bytes 9000000 | tf_op jit(solution)/shard_map/pallas_call | solution.py:278
  45.1 0.1 collective-permute-start.4
  45.2 7.2 %collective-permute-start.5 = (bf16[1024,128]{1,0:T(8,128)(2,1)S(1)}, bf16[1024,128]{1,0:T(8,128)(2,1)S(1)}, u32[]{:S(2)}, u32[]{:S(2)}) collective-permute-start(bf16[1024,128]{1,0:T(8,128)(2,1)S(1)} %get-tuple-element.39), channel_id=1, source_target_pairs={{0,127},{1,0},{2,1},{3,2},{4,3},{5,4},{6,5},{7,6},{8,7},{9,8},{10,... | collective-permute-start | bytes 786440 | tf_op jit(solution)/shard_map/ppermute | solution.py:219
  52.3 1.7 %shard_map.67.base = f32[1024,128]{1,0:T(8,128)S(1)} custom-call(bf16[1024,1024]{1,0:T(8,128)(2,1)S(1)} %get-tuple-element.32.sym, f32[1024,1]{1,0:T(8,128)S(1)} %copy.9.diag, bf16[1024,128]{1,0:T(8,128)(2,1)S(1)} %get-tuple-element.35.y.older, bf16[1024,128]{1,0:T(8,128)(2,1)} %older.1), custom_call_target="tpu_custom_call" | custom-call | flops 268435456 | bytes 3500000 | tf_op jit(solution)/shard_map/pallas_call | solution.py:284
  54.0 5.1 %collective-permute-done.4.got_left = bf16[1024,128]{1,0:T(8,128)(2,1)S(1)} collective-permute-done((bf16[1024,128]{1,0:T(8,128)(2,1)S(1)}, bf16[1024,128]{1,0:T(8,128)(2,1)S(1)}, u32[]{:S(2)}, u32[]{:S(2)}) %collective-permute-start.4) | collective-permute-done | bytes 262176 | tf_op jit(solution)/shard_map/ppermute | solution.py:219
  59.1 0.0 collective-permute-done.5.got_right
  59.1 2.2 %shard_map.68 = (bf16[1024,128]{1,0:T(8,128)(2,1)S(1)}, bf16[1024,128]{1,0:T(8,128)(2,1)S(1)}, bf16[1024,128]{1,0:T(8,128)(2,1)S(1)}) custom-call(f32[1024,128]{1,0:T(8,128)S(1)} %shard_map.67.base, bf16[1024,1024]{1,0:T(8,128)(2,1)S(1)} %get-tuple-element.36.edge, bf16[1024,1024]{1,0:T(8,128)(2,1)S(1)} %get-tuple-element.37.edge_t, ...), custom_call_target="tpu_custom_call" | custom-call | flops 536870912 | bytes 6000000 | tf_op jit(solution)/shard_map/pallas_call | solution.py:287
  61.4 0.1 collective-permute-start.6
  61.5 7.2 %collective-permute-start.7 = (bf16[1024,128]{1,0:T(8,128)(2,1)S(1)}, bf16[1024,128]{1,0:T(8,128)(2,1)S(1)}, u32[]{:S(2)}, u32[]{:S(2)}) collective-permute-start(bf16[1024,128]{1,0:T(8,128)(2,1)S(1)} %get-tuple-element.42), channel_id=1, source_target_pairs={{0,127},{1,0},{2,1},{3,2},{4,3},{5,4},{6,5},{7,6},{8,7},{9,8},{10,... | collective-permute-start | bytes 786440 | tf_op jit(solution)/shard_map/ppermute | solution.py:219
  68.6 0.7 shard_map.69.base
  69.3 5.3 %collective-permute-done.6.got_left = bf16[1024,128]{1,0:T(8,128)(2,1)S(1)} collective-permute-done((bf16[1024,128]{1,0:T(8,128)(2,1)S(1)}, bf16[1024,128]{1,0:T(8,128)(2,1)S(1)}, u32[]{:S(2)}, u32[]{:S(2)}) %collective-permute-start.6) | collective-permute-done | bytes 262176 | tf_op jit(solution)/shard_map/ppermute | solution.py:219
  74.6 0.0 collective-permute-done.7.got_right
  74.6 2.2 %shard_map.70 = (bf16[1024,128]{1,0:T(8,128)(2,1)S(1)}, bf16[1024,128]{1,0:T(8,128)(2,1)S(1)}, bf16[1024,128]{1,0:T(8,128)(2,1)S(1)}) custom-call(f32[1024,128]{1,0:T(8,128)S(1)} %shard_map.69.base, bf16[1024,1024]{1,0:T(8,128)(2,1)S(1)} %get-tuple-element.36.edge, bf16[1024,1024]{1,0:T(8,128)(2,1)S(1)} %get-tuple-element.37.edge_t, ...), custom_call_target="tpu_custom_call" | custom-call | flops 536870912 | bytes 6000000 | tf_op jit(solution)/shard_map/pallas_call | solution.py:287
  76.8 0.1 collective-permute-start.8
  76.9 7.2 %collective-permute-start.9 = (bf16[1024,128]{1,0:T(8,128)(2,1)S(1)}, bf16[1024,128]{1,0:T(8,128)(2,1)S(1)}, u32[]{:S(2)}, u32[]{:S(2)}) collective-permute-start(bf16[1024,128]{1,0:T(8,128)(2,1)S(1)} %get-tuple-element.45), channel_id=1, source_target_pairs={{0,127},{1,0},{2,1},{3,2},{4,3},{5,4},{6,5},{7,6},{8,7},{9,8},{10,... | collective-permute-start | bytes 786440 | tf_op jit(solution)/shard_map/ppermute | solution.py:219
  84.1 0.7 shard_map.71.base
  84.8 5.1 %collective-permute-done.8.got_left = bf16[1024,128]{1,0:T(8,128)(2,1)S(1)} collective-permute-done((bf16[1024,128]{1,0:T(8,128)(2,1)S(1)}, bf16[1024,128]{1,0:T(8,128)(2,1)S(1)}, u32[]{:S(2)}, u32[]{:S(2)}) %collective-permute-start.8) | collective-permute-done | bytes 262176 | tf_op jit(solution)/shard_map/ppermute | solution.py:219
  89.8 0.0 collective-permute-done.9.got_right
  89.8 2.2 %shard_map.72 = (bf16[1024,128]{1,0:T(8,128)(2,1)S(1)}, bf16[1024,128]{1,0:T(8,128)(2,1)S(1)}, bf16[1024,128]{1,0:T(8,128)(2,1)S(1)}) custom-call(f32[1024,128]{1,0:T(8,128)S(1)} %shard_map.71.base, bf16[1024,1024]{1,0:T(8,128)(2,1)S(1)} %get-tuple-element.36.edge, bf16[1024,1024]{1,0:T(8,128)(2,1)S(1)} %get-tuple-element.37.edge_t, ...), custom_call_target="tpu_custom_call" | custom-call | flops 536870912 | bytes 6000000 | tf_op jit(solution)/shard_map/pallas_call | solution.py:287
  92.1 0.1 collective-permute-start.10
  92.2 7.2 %collective-permute-start.11 = (bf16[1024,128]{1,0:T(8,128)(2,1)S(1)}, bf16[1024,128]{1,0:T(8,128)(2,1)S(1)}, u32[]{:S(2)}, u32[]{:S(2)}) collective-permute-start(bf16[1024,128]{1,0:T(8,128)(2,1)S(1)} %get-tuple-element.48), channel_id=1, source_target_pairs={{0,127},{1,0},{2,1},{3,2},{4,3},{5,4},{6,5},{7,6},{8,7},{9,8},{10,... | collective-permute-start | bytes 786440 | tf_op jit(solution)/shard_map/ppermute | solution.py:219
  99.3 0.7 shard_map.73.base
  100.0 4.7 %collective-permute-done.10.got_left = bf16[1024,128]{1,0:T(8,128)(2,1)S(1)} collective-permute-done((bf16[1024,128]{1,0:T(8,128)(2,1)S(1)}, bf16[1024,128]{1,0:T(8,128)(2,1)S(1)}, u32[]{:S(2)}, u32[]{:S(2)}) %collective-permute-start.10) | collective-permute-done | bytes 262176 | tf_op jit(solution)/shard_map/ppermute | solution.py:219
  104.7 0.0 collective-permute-done.11.got_right
  104.7 0.9 shard_map.74
  105.6 0.1 collective-permute-start.14
  105.7 0.1 collective-permute-start.13
  105.8 1.9 %collective-permute-start.12 = (f32[128,128]{1,0:T(8,128)S(1)}, f32[128,128]{1,0:T(8,128)S(1)}, u32[]{:S(2)}, u32[]{:S(2)}) collective-permute-start(f32[128,128]{1,0:T(8,128)S(1)} %get-tuple-element.49), channel_id=1, source_target_pairs={{0,1},{1,2},{2,3},{3,0},{4,5},{5,6},{6,7},{7,4},{8,9},{9,10},{10,1... | collective-permute-start | bytes 196616 | tf_op jit(solution)/shard_map/ppermute | solution.py:230
  107.7 2.2 %collective-permute-done.14 = f32[128,128]{1,0:T(8,128)S(1)} collective-permute-done((f32[128,128]{1,0:T(8,128)S(1)}, f32[128,128]{1,0:T(8,128)S(1)}, u32[]{:S(2)}, u32[]{:S(2)}) %collective-permute-start.14) | collective-permute-done | bytes 65568 | tf_op jit(solution)/shard_map/ppermute | solution.py:230
  109.9 1.6 %collective-permute-done.13 = f32[128,128]{1,0:T(8,128)S(1)} collective-permute-done((f32[128,128]{1,0:T(8,128)S(1)}, f32[128,128]{1,0:T(8,128)S(1)}, u32[]{:S(2)}, u32[]{:S(2)}) %collective-permute-start.13) | collective-permute-done | bytes 65568 | tf_op jit(solution)/shard_map/ppermute | solution.py:230
  111.5 1.1 collective-permute-done.12
  112.6 0.1 collective-permute-start.17
  112.7 0.1 collective-permute-start.16
  112.8 1.9 %collective-permute-start.15 = (f32[128,128]{1,0:T(8,128)S(1)}, f32[128,128]{1,0:T(8,128)S(1)}, u32[]{:S(2)}, u32[]{:S(2)}) collective-permute-start(f32[128,128]{1,0:T(8,128)S(1)} %add_add_fusion.2), channel_id=1, source_target_pairs={{0,4},{1,5},{2,6},{3,7},{4,8},{5,9},{6,10},{7,11},{8,12},{9,13},{1... | collective-permute-start | bytes 196616 | tf_op jit(solution)/shard_map/ppermute | solution.py:230
  114.7 2.2 %collective-permute-done.17 = f32[128,128]{1,0:T(8,128)S(1)} collective-permute-done((f32[128,128]{1,0:T(8,128)S(1)}, f32[128,128]{1,0:T(8,128)S(1)}, u32[]{:S(2)}, u32[]{:S(2)}) %collective-permute-start.17) | collective-permute-done | bytes 65568 | tf_op jit(solution)/shard_map/ppermute | solution.py:230
  117.0 1.6 %collective-permute-done.16 = f32[128,128]{1,0:T(8,128)S(1)} collective-permute-done((f32[128,128]{1,0:T(8,128)S(1)}, f32[128,128]{1,0:T(8,128)S(1)}, u32[]{:S(2)}, u32[]{:S(2)}) %collective-permute-start.16) | collective-permute-done | bytes 65568 | tf_op jit(solution)/shard_map/ppermute | solution.py:230
  118.6 1.1 collective-permute-done.15
  119.7 0.1 collective-permute-start.18
  119.8 1.2 collective-permute-done.18
  121.0 6.4 %collective-permute-start.21 = (f32[128,128]{1,0:T(8,128)S(1)}, f32[128,128]{1,0:T(8,128)S(1)}, u32[]{:S(2)}, u32[]{:S(2)}) collective-permute-start(f32[128,128]{1,0:T(8,128)S(1)} %add.68), channel_id=1, source_target_pairs={{0,96},{1,97},{2,98},{3,99},{4,100},{5,101},{6,102},{7,103},{8,104... | collective-permute-start | bytes 196616 | tf_op jit(solution)/shard_map/ppermute | solution.py:230
  127.4 0.0 collective-permute-start.20
  127.4 0.9 collective-permute-start.19
  128.3 2.2 %collective-permute-done.21 = f32[128,128]{1,0:T(8,128)S(1)} collective-permute-done((f32[128,128]{1,0:T(8,128)S(1)}, f32[128,128]{1,0:T(8,128)S(1)}, u32[]{:S(2)}, u32[]{:S(2)}) %collective-permute-start.21) | collective-permute-done | bytes 65568 | tf_op jit(solution)/shard_map/ppermute | solution.py:230
  130.5 3.0 %collective-permute-done.20 = f32[128,128]{1,0:T(8,128)S(1)} collective-permute-done((f32[128,128]{1,0:T(8,128)S(1)}, f32[128,128]{1,0:T(8,128)S(1)}, u32[]{:S(2)}, u32[]{:S(2)}) %collective-permute-start.20) | collective-permute-done | bytes 65568 | tf_op jit(solution)/shard_map/ppermute | solution.py:230
  133.5 0.4 collective-permute-done.19
  133.9 4.3 %shard_map.75 = f32[1024,128]{1,0:T(8,128)} custom-call(f32[128,128]{1,0:T(8,128)S(1)} %add_add_fusion.gram, bf16[1024,128]{1,0:T(8,128)(2,1)S(1)} %get-tuple-element.50.y), custom_call_target="tpu_custom_call" | custom-call | flops 536870912 | bytes 1000000 | tf_op jit(solution)/shard_map/pallas_call | solution.py:297
  (11 shorter events, 0.1 us)
Async XLA Ops:
  1.4 2.5 %copy-start = (bf16[4,10,256,256]{3,2,1,0:T(8,128)(2,1)S(1)}, bf16[4,10,256,256]{3,2,1,0:T(8,128)(2,1)}, u32[]{:S(2)}) copy-start(bf16[4,10,256,256]{3,2,1,0:T(8,128)(2,1)} %blocks.1) | copy-start | bytes 15728644
  3.9 0.7 copy-start.3
  4.6 16.4 %copy-start.4 = (f32[1024]{0:T(1024)S(1)}, f32[1024]{0:T(1024)}, u32[]{:S(2)}) copy-start(f32[1024]{0:T(1024)} %param.10) | copy-start | bytes 12292
  9.3 1.4 copy-start.1
  10.6 30.6 %collective-permute-start.2 = (bf16[2048,128]{1,0:T(8,128)(2,1)}, bf16[2048,128]{1,0:T(8,128)(2,1)}, u32[]{:S(2)}, u32[]{:S(2)}) collective-permute-start(bf16[2048,128]{1,0:T(8,128)(2,1)} %get-tuple-element.30.to_right), channel_id=1, source_target_pairs={{0,1},{1,2},{2,3},{3,4},{4,5},{5,6},{6,7},{7,8},{8,9},{9,10},{10,1... | collective-permute-start | bytes 1572872 | tf_op jit(solution)/shard_map/ppermute | solution.py:219
  12.4 28.8 %collective-permute-start.3 = (bf16[2048,128]{1,0:T(8,128)(2,1)}, bf16[2048,128]{1,0:T(8,128)(2,1)}, u32[]{:S(2)}, u32[]{:S(2)}) collective-permute-start(bf16[2048,128]{1,0:T(8,128)(2,1)} %get-tuple-element.31.to_left), channel_id=1, source_target_pairs={{0,127},{1,0},{2,1},{3,2},{4,3},{5,4},{6,5},{7,6},{8,7},{9,8},{10,... | collective-permute-start | bytes 1572872 | tf_op jit(solution)/shard_map/ppermute | solution.py:219
  18.9 15.9 %collective-permute-start.1 = (bf16[1024,128]{1,0:T(8,128)(2,1)}, bf16[1024,128]{1,0:T(8,128)(2,1)S(1)}, u32[]{:S(2)}, u32[]{:S(2)}) collective-permute-start(bf16[1024,128]{1,0:T(8,128)(2,1)} %older.1), channel_id=1, source_target_pairs={{0,127},{1,0},{2,1},{3,2},{4,3},{5,4},{6,5},{7,6},{8,7},{9,8},{10,... | collective-permute-start | bytes 786440 | tf_op jit(solution)/shard_map/ppermute | solution.py:219
  20.4 16.2 %collective-permute-start = (bf16[1024,128]{1,0:T(8,128)(2,1)}, bf16[1024,128]{1,0:T(8,128)(2,1)S(1)}, u32[]{:S(2)}, u32[]{:S(2)}) collective-permute-start(bf16[1024,128]{1,0:T(8,128)(2,1)} %older.1), channel_id=1, source_target_pairs={{0,1},{1,2},{2,3},{3,4},{4,5},{5,6},{6,7},{7,8},{8,9},{9,10},{10,1... | collective-permute-start | bytes 786440 | tf_op jit(solution)/shard_map/ppermute | solution.py:219
  36.7 1.6 %copy-start.2 = (bf16[1024,1024]{1,0:T(8,128)(2,1)S(1)}, bf16[1024,1024]{1,0:T(8,128)(2,1)}, u32[]{:S(2)}) copy-start(bf16[1024,1024]{1,0:T(8,128)(2,1)} %copy-done.1) | copy-start | bytes 6291460
  45.1 14.1 %collective-permute-start.4 = (bf16[1024,128]{1,0:T(8,128)(2,1)S(1)}, bf16[1024,128]{1,0:T(8,128)(2,1)S(1)}, u32[]{:S(2)}, u32[]{:S(2)}) collective-permute-start(bf16[1024,128]{1,0:T(8,128)(2,1)S(1)} %get-tuple-element.38), channel_id=1, source_target_pairs={{0,1},{1,2},{2,3},{3,4},{4,5},{5,6},{6,7},{7,8},{8,9},{9,10},{10,1... | collective-permute-start | bytes 786440 | tf_op jit(solution)/shard_map/ppermute | solution.py:219
  45.2 14.0 %collective-permute-start.5 = (bf16[1024,128]{1,0:T(8,128)(2,1)S(1)}, bf16[1024,128]{1,0:T(8,128)(2,1)S(1)}, u32[]{:S(2)}, u32[]{:S(2)}) collective-permute-start(bf16[1024,128]{1,0:T(8,128)(2,1)S(1)} %get-tuple-element.39), channel_id=1, source_target_pairs={{0,127},{1,0},{2,1},{3,2},{4,3},{5,4},{6,5},{7,6},{8,7},{9,8},{10,... | collective-permute-start | bytes 786440 | tf_op jit(solution)/shard_map/ppermute | solution.py:219
  61.4 13.2 %collective-permute-start.6 = (bf16[1024,128]{1,0:T(8,128)(2,1)S(1)}, bf16[1024,128]{1,0:T(8,128)(2,1)S(1)}, u32[]{:S(2)}, u32[]{:S(2)}) collective-permute-start(bf16[1024,128]{1,0:T(8,128)(2,1)S(1)} %get-tuple-element.41), channel_id=1, source_target_pairs={{0,1},{1,2},{2,3},{3,4},{4,5},{5,6},{6,7},{7,8},{8,9},{9,10},{10,1... | collective-permute-start | bytes 786440 | tf_op jit(solution)/shard_map/ppermute | solution.py:219
  61.5 13.1 %collective-permute-start.7 = (bf16[1024,128]{1,0:T(8,128)(2,1)S(1)}, bf16[1024,128]{1,0:T(8,128)(2,1)S(1)}, u32[]{:S(2)}, u32[]{:S(2)}) collective-permute-start(bf16[1024,128]{1,0:T(8,128)(2,1)S(1)} %get-tuple-element.42), channel_id=1, source_target_pairs={{0,127},{1,0},{2,1},{3,2},{4,3},{5,4},{6,5},{7,6},{8,7},{9,8},{10,... | collective-permute-start | bytes 786440 | tf_op jit(solution)/shard_map/ppermute | solution.py:219
  76.8 13.0 %collective-permute-start.8 = (bf16[1024,128]{1,0:T(8,128)(2,1)S(1)}, bf16[1024,128]{1,0:T(8,128)(2,1)S(1)}, u32[]{:S(2)}, u32[]{:S(2)}) collective-permute-start(bf16[1024,128]{1,0:T(8,128)(2,1)S(1)} %get-tuple-element.44), channel_id=1, source_target_pairs={{0,1},{1,2},{2,3},{3,4},{4,5},{5,6},{6,7},{7,8},{8,9},{9,10},{10,1... | collective-permute-start | bytes 786440 | tf_op jit(solution)/shard_map/ppermute | solution.py:219
  76.9 12.9 %collective-permute-start.9 = (bf16[1024,128]{1,0:T(8,128)(2,1)S(1)}, bf16[1024,128]{1,0:T(8,128)(2,1)S(1)}, u32[]{:S(2)}, u32[]{:S(2)}) collective-permute-start(bf16[1024,128]{1,0:T(8,128)(2,1)S(1)} %get-tuple-element.45), channel_id=1, source_target_pairs={{0,127},{1,0},{2,1},{3,2},{4,3},{5,4},{6,5},{7,6},{8,7},{9,8},{10,... | collective-permute-start | bytes 786440 | tf_op jit(solution)/shard_map/ppermute | solution.py:219
  92.1 12.6 %collective-permute-start.10 = (bf16[1024,128]{1,0:T(8,128)(2,1)S(1)}, bf16[1024,128]{1,0:T(8,128)(2,1)S(1)}, u32[]{:S(2)}, u32[]{:S(2)}) collective-permute-start(bf16[1024,128]{1,0:T(8,128)(2,1)S(1)} %get-tuple-element.47), channel_id=1, source_target_pairs={{0,1},{1,2},{2,3},{3,4},{4,5},{5,6},{6,7},{7,8},{8,9},{9,10},{10,1... | collective-permute-start | bytes 786440 | tf_op jit(solution)/shard_map/ppermute | solution.py:219
  92.2 12.5 %collective-permute-start.11 = (bf16[1024,128]{1,0:T(8,128)(2,1)S(1)}, bf16[1024,128]{1,0:T(8,128)(2,1)S(1)}, u32[]{:S(2)}, u32[]{:S(2)}) collective-permute-start(bf16[1024,128]{1,0:T(8,128)(2,1)S(1)} %get-tuple-element.48), channel_id=1, source_target_pairs={{0,127},{1,0},{2,1},{3,2},{4,3},{5,4},{6,5},{7,6},{8,7},{9,8},{10,... | collective-permute-start | bytes 786440 | tf_op jit(solution)/shard_map/ppermute | solution.py:219
  105.6 4.3 %collective-permute-start.14 = (f32[128,128]{1,0:T(8,128)S(1)}, f32[128,128]{1,0:T(8,128)S(1)}, u32[]{:S(2)}, u32[]{:S(2)}) collective-permute-start(f32[128,128]{1,0:T(8,128)S(1)} %get-tuple-element.49), channel_id=1, source_target_pairs={{0,3},{1,0},{2,1},{3,2},{4,7},{5,4},{6,5},{7,6},{8,11},{9,8},{10,9... | collective-permute-start | bytes 196616 | tf_op jit(solution)/shard_map/ppermute | solution.py:230
  105.7 5.8 %collective-permute-start.13 = (f32[128,128]{1,0:T(8,128)S(1)}, f32[128,128]{1,0:T(8,128)S(1)}, u32[]{:S(2)}, u32[]{:S(2)}) collective-permute-start(f32[128,128]{1,0:T(8,128)S(1)} %get-tuple-element.49), channel_id=1, source_target_pairs={{0,2},{1,3},{2,0},{3,1},{4,6},{5,7},{6,4},{7,5},{8,10},{9,11},{10,... | collective-permute-start | bytes 196616 | tf_op jit(solution)/shard_map/ppermute | solution.py:230
  105.8 6.8 %collective-permute-start.12 = (f32[128,128]{1,0:T(8,128)S(1)}, f32[128,128]{1,0:T(8,128)S(1)}, u32[]{:S(2)}, u32[]{:S(2)}) collective-permute-start(f32[128,128]{1,0:T(8,128)S(1)} %get-tuple-element.49), channel_id=1, source_target_pairs={{0,1},{1,2},{2,3},{3,0},{4,5},{5,6},{6,7},{7,4},{8,9},{9,10},{10,1... | collective-permute-start | bytes 196616 | tf_op jit(solution)/shard_map/ppermute | solution.py:230
  112.6 4.3 %collective-permute-start.17 = (f32[128,128]{1,0:T(8,128)S(1)}, f32[128,128]{1,0:T(8,128)S(1)}, u32[]{:S(2)}, u32[]{:S(2)}) collective-permute-start(f32[128,128]{1,0:T(8,128)S(1)} %add_add_fusion.2), channel_id=1, source_target_pairs={{0,12},{1,13},{2,14},{3,15},{4,0},{5,1},{6,2},{7,3},{8,4},{9,5},{1... | collective-permute-start | bytes 196616 | tf_op jit(solution)/shard_map/ppermute | solution.py:230
  112.7 5.8 %collective-permute-start.16 = (f32[128,128]{1,0:T(8,128)S(1)}, f32[128,128]{1,0:T(8,128)S(1)}, u32[]{:S(2)}, u32[]{:S(2)}) collective-permute-start(f32[128,128]{1,0:T(8,128)S(1)} %add_add_fusion.2), channel_id=1, source_target_pairs={{0,8},{1,9},{2,10},{3,11},{4,12},{5,13},{6,14},{7,15},{8,0},{9,1},... | collective-permute-start | bytes 196616 | tf_op jit(solution)/shard_map/ppermute | solution.py:230
  112.8 6.8 %collective-permute-start.15 = (f32[128,128]{1,0:T(8,128)S(1)}, f32[128,128]{1,0:T(8,128)S(1)}, u32[]{:S(2)}, u32[]{:S(2)}) collective-permute-start(f32[128,128]{1,0:T(8,128)S(1)} %add_add_fusion.2), channel_id=1, source_target_pairs={{0,4},{1,5},{2,6},{3,7},{4,8},{5,9},{6,10},{7,11},{8,12},{9,13},{1... | collective-permute-start | bytes 196616 | tf_op jit(solution)/shard_map/ppermute | solution.py:230
  119.7 1.3 collective-permute-start.18
  121.0 9.5 %collective-permute-start.21 = (f32[128,128]{1,0:T(8,128)S(1)}, f32[128,128]{1,0:T(8,128)S(1)}, u32[]{:S(2)}, u32[]{:S(2)}) collective-permute-start(f32[128,128]{1,0:T(8,128)S(1)} %add.68), channel_id=1, source_target_pairs={{0,96},{1,97},{2,98},{3,99},{4,100},{5,101},{6,102},{7,103},{8,104... | collective-permute-start | bytes 196616 | tf_op jit(solution)/shard_map/ppermute | solution.py:230
  127.4 6.1 %collective-permute-start.20 = (f32[128,128]{1,0:T(8,128)S(1)}, f32[128,128]{1,0:T(8,128)S(1)}, u32[]{:S(2)}, u32[]{:S(2)}) collective-permute-start(f32[128,128]{1,0:T(8,128)S(1)} %add.68), channel_id=1, source_target_pairs={{0,64},{1,65},{2,66},{3,67},{4,68},{5,69},{6,70},{7,71},{8,72},{9,... | collective-permute-start | bytes 196616 | tf_op jit(solution)/shard_map/ppermute | solution.py:230
  127.4 6.5 %collective-permute-start.19 = (f32[128,128]{1,0:T(8,128)S(1)}, f32[128,128]{1,0:T(8,128)S(1)}, u32[]{:S(2)}, u32[]{:S(2)}) collective-permute-start(f32[128,128]{1,0:T(8,128)S(1)} %add.68), channel_id=1, source_target_pairs={{0,32},{1,33},{2,34},{3,35},{4,36},{5,37},{6,38},{7,39},{8,40},{9,... | collective-permute-start | bytes 196616 | tf_op jit(solution)/shard_map/ppermute | solution.py:230

commit v2 on v1

--- a/solution.py
+++ b/solution.py
@@ -43,41 +43,78 @@
     return block.astype(F32).T
 
 
-def prep_kernel(weight, offset, live, blocks, y0, own, edge, to_right, to_left, buf, acc, sem):
+def prep_kernel(total, scales, columns, live, blocks, y0, own, edge, to_right, to_left, buf, acc, head, after, sem):
     copies = [pltpu.make_async_copy(blocks.at[a], buf.at[a], sem.at[a]) for a in range(ROWS)]
     for copy in copies:
         copy.start()
-    for a in range(ROWS):
-        acc[...] = jnp.zeros_like(acc)
-        copies[a].wait()
-
-        def add_slot(s, carry, a=a):
-            o = offset[a, s]
-            acc[o] = acc[o] + weight[a, s] * buf[a, s].astype(F32)
+    first = lax.axis_index(AXES) * ROWS
+    for a in range(ROWS):
+        for o in range(SPAN):
+            head[a, o] = -1
+
+        def chain(s, carry, a=a):
+            o = lax.rem(columns[a, s] - (first + a) + REACH + total, total)
+            after[a, s] = head[a, o]
+            head[a, o] = s
             return carry
 
-        lax.fori_loop(0, live[a], add_slot, 0)
-        for o in range(SPAN):
-            p = a + o
-            value = acc[o].astype(BF16)
-            if 4 <= p < 8:
-                own[rows(a), rows(p - 4)] = value
-            elif p in EDGE:
-                edge[rows(a), rows(EDGE.index(p))] = value
-            else:
-                places, target = (TO_RIGHT, to_right) if p > 8 else (TO_LEFT, to_left)
-                i = places.index((a, p))
-                target[rows(2 * i), :] = value[:, :K]
-                target[rows(2 * i + 1), :] = value[:, K:]
+        lax.fori_loop(0, live[a], chain, 0)
+    turned = flip(y0[...]).astype(BF16)
+    for target in (to_right, to_left):
+        target[pl.ds(HANDED + 2 * B, OWN), :] = y0[...]
+
+    def put(a, p, value):
+        if 4 <= p < 8:
+            own[rows(a), rows(p - 4)] = value
+        elif p in EDGE:
+            edge[rows(a), rows(EDGE.index(p))] = value
+        else:
+            places, target = (TO_RIGHT, to_right) if p > 8 else (TO_LEFT, to_left)
+            i = places.index((a, p))
+            target[rows(2 * i), :] = value[:, :K]
+            target[rows(2 * i + 1), :] = value[:, K:]
+
+    def scaled(a, s):
+        return (scales[a, s] * ALPHA) * buf[a, s].astype(F32)
+
+    def place(a, o):
+        s = head[a, o]
+
+        @pl.when(s < 0)
+        def _():
+            put(a, a + o, jnp.zeros((B, B), BF16))
+
+        @pl.when(s >= 0)
+        def _():
+            rest = after[a, jnp.maximum(s, 0)]
+
+            @pl.when(rest < 0)
+            def _():
+                put(a, a + o, scaled(a, s).astype(BF16))
+
+            @pl.when(rest >= 0)
+            def _():
+                acc[...] = scaled(a, s)
+
+                def more(t):
+                    acc[...] = acc[...] + scaled(a, t)
+                    return after[a, t]
+
+                lax.while_loop(lambda t: t >= 0, more, rest)
+                put(a, a + o, acc[...].astype(BF16))
+
     edge[rows(0), rows(1)] = jnp.zeros((B, B), BF16)
     edge[rows(3), rows(2)] = jnp.zeros((B, B), BF16)
-    turned = flip(y0[...]).astype(BF16)
+    for a in range(ROWS):
+        copies[a].wait()
+        for o in range(SPAN):
+            place(a, o)
     terms = dot(turned, edge[...]).T.astype(BF16)
     to_right[pl.ds(HANDED, 2 * B), :] = terms[: 2 * B]
     to_left[pl.ds(HANDED, 2 * B), :] = terms[2 * B :]
 
 
-def first_local_kernel(own, edge, diag, y0, left, right, to_right, to_left, sym, edge_t, base):
+def first_local_kernel(own, edge, onsite, y0, diag, sym, edge_t, base):
     for a in range(ROWS):
         for b in range(a + 1):
             value = own[rows(a), rows(b)].astype(F32) + flip(own[rows(b), rows(a)])
@@ -87,20 +124,32 @@
     for a in range(ROWS):
         for j in range(4):
             edge_t[rows(j), rows(a)] = flip(edge[rows(a), rows(j)]).astype(BF16)
+    diag[...] = ALPHA * (onsite[...] - SHIFT)
     base[...] = diag[...] * y0[...].astype(F32) + dot(sym[...], y0[...])
-    for places, source, halo, first in ((TO_LEFT, to_left, left, 0), (TO_RIGHT, to_right, right, 8)):
-        for i, (a, p) in enumerate(places):
-            base[rows(a), :] += dot(read_block(source, i), halo[rows(p - first), :])
-
-
-def send_parts(y, terms, send_right, send_left):
-    send_right[pl.ds(0, 2 * B), :] = y[2 * B :]
-    send_right[pl.ds(2 * B, 2 * B), :] = terms[: 2 * B]
-    send_left[pl.ds(0, 2 * B), :] = y[: 2 * B]
-    send_left[pl.ds(2 * B, 2 * B), :] = terms[2 * B :]
-
-
-def first_post_kernel(base, edge_in, edge_t_in, left, right, got_left, got_right, edge, edge_t, y_out, send_right, send_left):
+
+
+def forward(a, base, edge, right, left):
+    wide = 1 if a == 0 else 2
+    skip = 1 if a == ROWS - 1 else 0
+    total = base[rows(a), :] + dot(edge[rows(a), rows(0, wide)], right(0, wide))
+    return total + dot(edge[rows(a), rows(2 + skip, 2 - skip)], left(skip, 2 - skip))
+
+
+def terms_of(a, got_left, got_right, start):
+    got = got_left if a < 2 else got_right
+    return got[pl.ds(start + (a % 2) * B, B), :].astype(F32)
+
+
+def send_parts(edge_t, y, send_right, send_left):
+    send_right[pl.ds(0, 2 * B), :] = y[pl.ds(2 * B, 2 * B), :]
+    send_left[pl.ds(0, 2 * B), :] = y[pl.ds(0, 2 * B), :]
+    send_right[pl.ds(2 * B, B), :] = dot(edge_t[rows(0), :], y[...]).astype(BF16)
+    send_right[pl.ds(3 * B, B), :] = dot(edge_t[rows(1), rows(1, 3)], y[rows(1, 3), :]).astype(BF16)
+    send_left[pl.ds(2 * B, B), :] = dot(edge_t[rows(2), rows(0, 3)], y[rows(0, 3), :]).astype(BF16)
+    send_left[pl.ds(3 * B, B), :] = dot(edge_t[rows(3), :], y[...]).astype(BF16)
+
+
+def first_post_kernel(base, edge_in, edge_t_in, to_right, to_left, got_left, got_right, edge, edge_t, y, send_right, send_left):
     edge[...] = edge_in[...]
     edge_t[...] = edge_t_in[...]
     for i, (r, c) in enumerate(TO_LEFT):
@@ -112,30 +161,44 @@
         r = p - 8
         edge_t[rows(c), rows(r)] = (edge_t[rows(c), rows(r)].astype(F32) + block).astype(BF16)
         edge[rows(r), rows(c)] = (edge[rows(r), rows(c)].astype(F32) + block.T).astype(BF16)
-    halo = jnp.concatenate([right[pl.ds(0, 2 * B), :], left[pl.ds(2 * B, 2 * B), :]], axis=0)
-    terms = jnp.concatenate([got_left[pl.ds(HANDED, 2 * B), :], got_right[pl.ds(HANDED, 2 * B), :]], axis=0)
-    total = base[...] + dot(edge[...], halo) + terms.astype(F32)
-    y = (0.5 * total).astype(BF16)
-    y_out[...] = y
-    send_parts(y, dot(edge_t[...], y).astype(BF16), send_right, send_left)
-
-
-def received(base, edge, got_left, got_right):
-    halo = jnp.concatenate([got_right[pl.ds(0, 2 * B), :], got_left[pl.ds(0, 2 * B), :]], axis=0)
-    terms = jnp.concatenate([got_left[pl.ds(2 * B, 2 * B), :], got_right[pl.ds(2 * B, 2 * B), :]], axis=0)
-    return (base[...] + dot(edge[...], halo) + terms.astype(F32)).astype(BF16)
-
-
-def post_kernel(base, edge, edge_t, got_left, got_right, y_out, send_right, send_left):
-    y = received(base, edge, got_left, got_right)
-    y_out[...] = y
-    send_parts(y, dot(edge_t[...], y).astype(BF16), send_right, send_left)
-
-
-def last_kernel(base, edge, got_left, got_right, y_out, gram):
-    y = received(base, edge, got_left, got_right)
-    y_out[...] = y
-    gram[...] = lax.dot_general(y, y, (((0,), (0,)), ((), ())), preferred_element_type=F32)
+    halo = HANDED + 2 * B
+
+    def right(i, n):
+        return got_right[pl.ds(halo + i * B, n * B), :]
+
+    def left(i, n):
+        return got_left[pl.ds(halo + (2 + i) * B, n * B), :]
+
+    for a in range(ROWS):
+        total = forward(a, base, edge, right, left) + terms_of(a, got_left, got_right, HANDED)
+        for places, source, got, start in ((TO_LEFT, to_left, got_left, 0), (TO_RIGHT, to_right, got_right, 8)):
+            for i, (row, p) in enumerate(places):
+                if row == a:
+                    total += dot(read_block(source, i), got[pl.ds(halo + (p - start) * B, B), :])
+        y[rows(a), :] = (0.5 * total).astype(BF16)
+    send_parts(edge_t, y, send_right, send_left)
+
+
+def receive(base, edge, got_left, got_right, y):
+    def right(i, n):
+        return got_right[rows(i, n), :]
+
+    def left(i, n):
+        return got_left[rows(i, n), :]
+
+    for a in range(ROWS):
+        total = forward(a, base, edge, right, left) + terms_of(a, got_left, got_right, 2 * B)
+        y[rows(a), :] = total.astype(BF16)
+
+
+def post_kernel(base, edge, edge_t, got_left, got_right, y, send_right, send_left):
+    receive(base, edge, got_left, got_right, y)
+    send_parts(edge_t, y, send_right, send_left)
+
+
+def last_kernel(base, edge, got_left, got_right, y, gram):
+    receive(base, edge, got_left, got_right, y)
+    gram[...] = lax.dot_general(y[...], y[...], (((0,), (0,)), ((), ())), preferred_element_type=F32)
 
 
 def local_kernel(sym, diag, y, older, base):
@@ -197,8 +260,8 @@
 
 VMEM = pl.BlockSpec(memory_space=pltpu.VMEM)
 SMEM = pl.BlockSpec(memory_space=pltpu.SMEM)
-ANY = pl.BlockSpec(memory_space=pl.ANY)
-LIMIT = 32 * 1024 * 1024
+HBM = pl.BlockSpec(memory_space=pltpu.HBM)
+LIMIT = 20 * 1024 * 1024
 
 
 def call(kernel, outs, specs, flops, size, scratch=(), aliases=None):
@@ -226,7 +289,8 @@
         pairs = []
         for i in range(count):
             digit = (i // stride) % size
-            pairs.append((i, i + ((digit + step) % size - digit) * stride))
+            partner = digit ^ step if size & (size - 1) == 0 else (digit + step) % size
+            pairs.append((i, i + (partner - digit) * stride))
         parts.append(lax.ppermute(value, AXES, pairs))
     return sum(parts[1:], parts[0])
 
@@ -247,37 +311,35 @@
 def local(blocks, block_scales, columns, live, onsite, start_vectors):
     slots = columns.shape[1]
     total = ROWS * lax.axis_size(AXES)
-    row_ids = lax.axis_index(AXES) * ROWS + jnp.arange(ROWS, dtype=jnp.int32)
-    offset = (columns - row_ids[:, None] + REACH) % total
-    weight = block_scales * ALPHA
-    diag = (ALPHA * (onsite - SHIFT))[:, None]
+    column = ((OWN, 1), F32)
     tall = ((OWN, K), BF16)
     tall32 = ((OWN, K), F32)
     square = ((OWN, OWN), BF16)
-    handed = ((HANDED + 2 * B, K), BF16)
+    message = ((HANDED + 2 * B + OWN, K), BF16)
     product = 2 * OWN * OWN * K
 
     y0 = start_vectors
-    left, right = ring(y0, 1), ring(y0, -1)
     own, edge, to_right, to_left = call(
-        prep_kernel,
-        [square, square, handed, handed],
-        [SMEM, SMEM, SMEM, ANY, VMEM],
+        functools.partial(prep_kernel, total),
+        [square, square, message, message],
+        [SMEM, SMEM, SMEM, HBM, VMEM],
         product,
         10_000_000,
         [
             pltpu.VMEM((ROWS, slots, B, B), BF16),
-            pltpu.VMEM((SPAN, B, B), F32),
+            pltpu.VMEM((B, B), F32),
+            pltpu.SMEM((ROWS, SPAN), jnp.int32),
+            pltpu.SMEM((ROWS, slots), jnp.int32),
             pltpu.SemaphoreType.DMA((ROWS,)),
         ],
-    )(weight, offset, live, blocks, y0)
+    )(block_scales, columns, live, blocks, y0)
     got_left, got_right = ring(to_right, 1), ring(to_left, -1)
-    sym, edge_t, base = call(first_local_kernel, [square, square, tall32], [VMEM] * 8, product, 10_000_000)(
-        own, edge, diag, y0, left, right, to_right, to_left
+    diag, sym, edge_t, base = call(first_local_kernel, [column, square, square, tall32], [VMEM] * 4, product, 10_000_000)(
+        own, edge, onsite[:, None], y0
     )
     edge, edge_t, y, send_right, send_left = call(
         first_post_kernel, [square, square, tall, tall, tall], [VMEM] * 7, 2 * product, 9_000_000, (), {1: 0, 2: 1}
-    )(base, edge, edge_t, left, right, got_left, got_right)
+    )(base, edge, edge_t, to_right, to_left, got_left, got_right)
     older = y0
     for step in range(1, DEG):
         got_left, got_right = ring(send_right, 1), ring(send_left, -1)

time: 138 us -> 127 us (0.920); the launches traced: 138 us -> 130 us
  Pallas kernels: 27.1 us -> 22.2 us
  waiting for transfers between devices: 52.2 us -> 48.2 us
  local copies, waits for them, and re-layouts: 6.31 us -> 8.6 us
  other arithmetic: 1.51 us -> 0.06 us
    ppermute x10, waiting for transfers between devices: 16.6 us -> 12.3 us  [group_sum(): parts.append(lax.ppermute(value, AXES, pairs))]
    pallas_call x3, Pallas kernels: 6.7 us -> 3.81 us  [local(): call(post_kernel, [tall, tall, tall], [VMEM] * 5, 2 * product, 6000000)]
    unnamed x10 -> x18, local copies, waits for them, and re-layouts: 6.08 us -> 8.38 us
    ppermute x12 -> x10, starting transfers between devices: 39.3 us -> 37.1 us  [ring(): lax.ppermute(value, AXES, [(i, (i + step) % count) for i in range(count)])]
    ppermute x10, starting transfers between devices: 11.6 us -> 13.1 us  [group_sum(): parts.append(lax.ppermute(value, AXES, pairs))]
    ppermute x12 -> x10, waiting for transfers between devices: 35.6 us -> 36 us  [ring(): lax.ppermute(value, AXES, [(i, (i + step) % count) for i in range(count)])]
  transfers between devices with their start and end apart: 22 -> 20, of which waited for: 16 -> 12; matrix products, arithmetic and copies ran while one was open for 0% -> 0% of each run, Pallas kernels for 5% -> 3%
where the time goes in v2:
time: 127 us; the launch traced here: 130 us
  starting transfers between devices  50.3 us (40%)
  waiting for transfers between devices  48.2 us (38%)
  Pallas kernels  22.2 us (17%)
  local copies, waits for them, and re-layouts  8.6 us (7%)
    ppermute x10, starting transfers between devices, ring(): lax.ppermute(value, AXES, [(i, (i + step) % count) for i in range(count)])  37.1 us
    ppermute x10, waiting for transfers between devices, ring(): lax.ppermute(value, AXES, [(i, (i + step) % count) for i in range(count)])  36 us
    ppermute x10, starting transfers between devices, group_sum(): parts.append(lax.ppermute(value, AXES, pairs))  13.1 us
    ppermute x10, waiting for transfers between devices, group_sum(): parts.append(lax.ppermute(value, AXES, pairs))  12.3 us
    unnamed x18, local copies, waits for them, and re-layouts  8.38 us
    pallas_call x1, Pallas kernels, local(): call(functools.partial(prep_kernel, total), [square, square, message, mes...  4.61 us
    pallas_call x1, Pallas kernels, local(): call(functools.partial(finish_kernel, scale), [tall32], [VMEM] * 2, 2 * p...  4.27 us
    pallas_call x1, Pallas kernels, local(): call(first_post_kernel, [square, square, tall, tall, tall], [VMEM] * 7, 2...  4.14 us
  transfers between devices with their start and end apart: 20, of which 12 were waited for; matrix products, arithmetic and copies ran while one was open for 0% of the time, Pallas kernels for 3%

profile of v2, /device:TPU:0, one launch (start us, length us, event | category | flops | bytes accessed | tf_op | source)
XLA Modules:
  0.0 129.5 jit_solution(3250908149771697591)
XLA Ops:
  0.0 2.5 %copy-done = bf16[4,10,256,256]{3,2,1,0:T(8,128)(2,1)S(1)} copy-done((bf16[4,10,256,256]{3,2,1,0:T(8,128)(2,1)S(1)}, bf16[4,10,256,256]{3,2,1,0:T(8,128)(2,1)}, u32[]{:S(2)}) %copy-start) | copy-done | bytes 5242904
  2.5 0.9 copy-done.1
  3.4 0.7 copy-done.5
  4.1 0.7 copy-done.6
  4.8 0.7 copy-done.7
  5.5 4.6 %shard_map.64 = (bf16[1024,1024]{1,0:T(8,128)(2,1)S(1)}, bf16[1024,1024]{1,0:T(8,128)(2,1)S(1)}, bf16[3072,128]{1,0:T(8,128)(2,1)}, bf16[3072,128]{1,0:T(8,128)(2,1)}) custom-call(f32[4,10]{1,0:T(4,128)S(1)} %copy-done.5, s32[4,10]{1,0:T(4,128)S(1)} %copy-done.6, s32[4]{0:T(128)S(1)} %copy-done.7, bf16[4,10,256,256]{3,2,1,0:T(8,128)(2,1)S(1)} %copy-done, ...), custom_call_target="tpu_custom_call" | custom-call | flops 268435456 | bytes 10000000 | tf_op jit(solution)/shard_map/pallas_call | solution.py:322
  10.1 0.0 copy-start.3
  10.1 1.3 %copy-done.3 = bf16[1024,1024]{1,0:T(8,128)(2,1)} copy-done((bf16[1024,1024]{1,0:T(8,128)(2,1)}, bf16[1024,1024]{1,0:T(8,128)(2,1)S(1)}, u32[]{:S(2)}) %copy-start.3) | copy-done | bytes 2097176
  11.4 1.7 %collective-permute-start = (bf16[3072,128]{1,0:T(8,128)(2,1)}, bf16[3072,128]{1,0:T(8,128)(2,1)}, u32[]{:S(2)}, u32[]{:S(2)}) collective-permute-start(bf16[3072,128]{1,0:T(8,128)(2,1)} %get-tuple-element.35.to_right), channel_id=1, source_target_pairs={{0,1},{1,2},{2,3},{3,4},{4,5},{5,6},{6,7},{7,8},{8,9},{9,10},{10,1... | collective-permute-start | bytes 2359304 | tf_op jit(solution)/shard_map/ppermute | solution.py:282
  13.2 6.4 %collective-permute-start.1 = (bf16[3072,128]{1,0:T(8,128)(2,1)}, bf16[3072,128]{1,0:T(8,128)(2,1)}, u32[]{:S(2)}, u32[]{:S(2)}) collective-permute-start(bf16[3072,128]{1,0:T(8,128)(2,1)} %get-tuple-element.36.to_left), channel_id=1, source_target_pairs={{0,127},{1,0},{2,1},{3,2},{4,3},{5,4},{6,5},{7,6},{8,7},{9,8},{10,... | collective-permute-start | bytes 2359304 | tf_op jit(solution)/shard_map/ppermute | solution.py:282
  19.6 0.0 copy-done.8
  19.6 0.2 copy.9.onsite
  19.8 0.0 copy-done.2
  19.8 0.0 copy-start.4
  19.9 1.6 %copy-done.4 = bf16[1024,1024]{1,0:T(8,128)(2,1)S(1)} copy-done((bf16[1024,1024]{1,0:T(8,128)(2,1)S(1)}, bf16[1024,1024]{1,0:T(8,128)(2,1)}, u32[]{:S(2)}) %copy-start.4) | copy-done | bytes 2097176
  21.4 1.6 %shard_map.65 = (f32[1024,1]{1,0:T(8,128)S(1)}, bf16[1024,1024]{1,0:T(8,128)(2,1)S(1)}, bf16[1024,1024]{1,0:T(8,128)(2,1)S(1)}, f32[1024,128]{1,0:T(8,128)S(1)}) custom-call(bf16[1024,1024]{1,0:T(8,128)(2,1)S(1)} %copy-done.4, bf16[1024,1024]{1,0:T(8,128)(2,1)S(1)} %get-tuple-element.30.edge.edge_in, f32[1024,1]{1,0:T(8,128)S(1)} %copy.9.onsite, ...), custom_call_target="tpu_custom_call" | custom-call | flops 268435456 | bytes 10000000 | tf_op jit(solution)/shard_map/pallas_call | solution.py:337
  23.1 14.4 %collective-permute-done.got_left = bf16[3072,128]{1,0:T(8,128)(2,1)} collective-permute-done((bf16[3072,128]{1,0:T(8,128)(2,1)}, bf16[3072,128]{1,0:T(8,128)(2,1)}, u32[]{:S(2)}, u32[]{:S(2)}) %collective-permute-start) | collective-permute-done | bytes 786464 | tf_op jit(solution)/shard_map/ppermute | solution.py:282
  37.4 0.0 collective-permute-done.1.got_right
  37.4 4.1 %shard_map.66 = (bf16[1024,1024]{1,0:T(8,128)(2,1)S(1)}, bf16[1024,1024]{1,0:T(8,128)(2,1)S(1)}, bf16[1024,128]{1,0:T(8,128)(2,1)S(1)}, bf16[1024,128]{1,0:T(8,128)(2,1)S(1)}, bf16[1024,128]{1,0:T(8,128)(2,1)S(1)}) custom-call(f32[1024,128]{1,0:T(8,128)S(1)} %get-tuple-element.33.base, ...), custom_call_target="tpu_custom_call", output_to_operand_aliasing={{0}: (1, {}), {1}: (2, {})} | custom-call | flops 536870912 | bytes 9000000 | tf_op jit(solution)/shard_map/pallas_call | solution.py:340
  41.6 0.1 collective-permute-start.2
  41.7 7.2 %collective-permute-start.3 = (bf16[1024,128]{1,0:T(8,128)(2,1)S(1)}, bf16[1024,128]{1,0:T(8,128)(2,1)S(1)}, u32[]{:S(2)}, u32[]{:S(2)}) collective-permute-start(bf16[1024,128]{1,0:T(8,128)(2,1)S(1)} %get-tuple-element.41), channel_id=1, source_target_pairs={{0,127},{1,0},{2,1},{3,2},{4,3},{5,4},{6,5},{7,6},{8,7},{9,8},{10,... | collective-permute-start | bytes 786440 | tf_op jit(solution)/shard_map/ppermute | solution.py:282
  48.8 0.7 shard_map.67.base
  49.5 5.6 %collective-permute-done.2.got_left = bf16[1024,128]{1,0:T(8,128)(2,1)S(1)} collective-permute-done((bf16[1024,128]{1,0:T(8,128)(2,1)S(1)}, bf16[1024,128]{1,0:T(8,128)(2,1)S(1)}, u32[]{:S(2)}, u32[]{:S(2)}) %collective-permute-start.2) | collective-permute-done | bytes 262176 | tf_op jit(solution)/shard_map/ppermute | solution.py:282
  55.1 0.0 collective-permute-done.3.got_right
  55.1 1.3 shard_map.68
  56.4 0.1 collective-permute-start.4
  56.5 7.2 %collective-permute-start.5 = (bf16[1024,128]{1,0:T(8,128)(2,1)S(1)}, bf16[1024,128]{1,0:T(8,128)(2,1)S(1)}, u32[]{:S(2)}, u32[]{:S(2)}) collective-permute-start(bf16[1024,128]{1,0:T(8,128)(2,1)S(1)} %get-tuple-element.44), channel_id=1, source_target_pairs={{0,127},{1,0},{2,1},{3,2},{4,3},{5,4},{6,5},{7,6},{8,7},{9,8},{10,... | collective-permute-start | bytes 786440 | tf_op jit(solution)/shard_map/ppermute | solution.py:282
  63.7 0.7 shard_map.69.base
  64.4 5.9 %collective-permute-done.4.got_left = bf16[1024,128]{1,0:T(8,128)(2,1)S(1)} collective-permute-done((bf16[1024,128]{1,0:T(8,128)(2,1)S(1)}, bf16[1024,128]{1,0:T(8,128)(2,1)S(1)}, u32[]{:S(2)}, u32[]{:S(2)}) %collective-permute-start.4) | collective-permute-done | bytes 262176 | tf_op jit(solution)/shard_map/ppermute | solution.py:282
  70.2 0.0 collective-permute-done.5.got_right
  70.2 1.3 shard_map.70
  71.5 0.1 collective-permute-start.6
  71.6 7.2 %collective-permute-start.7 = (bf16[1024,128]{1,0:T(8,128)(2,1)S(1)}, bf16[1024,128]{1,0:T(8,128)(2,1)S(1)}, u32[]{:S(2)}, u32[]{:S(2)}) collective-permute-start(bf16[1024,128]{1,0:T(8,128)(2,1)S(1)} %get-tuple-element.47), channel_id=1, source_target_pairs={{0,127},{1,0},{2,1},{3,2},{4,3},{5,4},{6,5},{7,6},{8,7},{9,8},{10,... | collective-permute-start | bytes 786440 | tf_op jit(solution)/shard_map/ppermute | solution.py:282
  78.8 0.7 shard_map.71.base
  79.5 5.8 %collective-permute-done.6.got_left = bf16[1024,128]{1,0:T(8,128)(2,1)S(1)} collective-permute-done((bf16[1024,128]{1,0:T(8,128)(2,1)S(1)}, bf16[1024,128]{1,0:T(8,128)(2,1)S(1)}, u32[]{:S(2)}, u32[]{:S(2)}) %collective-permute-start.6) | collective-permute-done | bytes 262176 | tf_op jit(solution)/shard_map/ppermute | solution.py:282
  85.2 0.0 collective-permute-done.7.got_right
  85.2 1.3 shard_map.72
  86.5 0.1 collective-permute-start.8
  86.6 7.2 %collective-permute-start.9 = (bf16[1024,128]{1,0:T(8,128)(2,1)S(1)}, bf16[1024,128]{1,0:T(8,128)(2,1)S(1)}, u32[]{:S(2)}, u32[]{:S(2)}) collective-permute-start(bf16[1024,128]{1,0:T(8,128)(2,1)S(1)} %get-tuple-element.50), channel_id=1, source_target_pairs={{0,127},{1,0},{2,1},{3,2},{4,3},{5,4},{6,5},{7,6},{8,7},{9,8},{10,... | collective-permute-start | bytes 786440 | tf_op jit(solution)/shard_map/ppermute | solution.py:282
  93.8 0.7 shard_map.73.base
  94.5 4.4 %collective-permute-done.8.got_left = bf16[1024,128]{1,0:T(8,128)(2,1)S(1)} collective-permute-done((bf16[1024,128]{1,0:T(8,128)(2,1)S(1)}, bf16[1024,128]{1,0:T(8,128)(2,1)S(1)}, u32[]{:S(2)}, u32[]{:S(2)}) %collective-permute-start.8) | collective-permute-done | bytes 262176 | tf_op jit(solution)/shard_map/ppermute | solution.py:282
  98.9 0.0 collective-permute-done.9.got_right
  98.9 0.9 shard_map.74
  99.8 0.1 collective-permute-start.12
  99.9 0.1 collective-permute-start.11
  100.0 4.0 %collective-permute-start.10 = (f32[128,128]{1,0:T(8,128)S(1)}, f32[128,128]{1,0:T(8,128)S(1)}, u32[]{:S(2)}, u32[]{:S(2)}) collective-permute-start(f32[128,128]{1,0:T(8,128)S(1)} %get-tuple-element.51), channel_id=1, source_target_pairs={{0,1},{1,0},{2,3},{3,2},{4,5},{5,4},{6,7},{7,6},{8,9},{9,8},{10,11... | collective-permute-start | bytes 196616 | tf_op jit(solution)/shard_map/ppermute | solution.py:294
  104.0 2.1 %collective-permute-done.12 = f32[128,128]{1,0:T(8,128)S(1)} collective-permute-done((f32[128,128]{1,0:T(8,128)S(1)}, f32[128,128]{1,0:T(8,128)S(1)}, u32[]{:S(2)}, u32[]{:S(2)}) %collective-permute-start.12) | collective-permute-done | bytes 65568 | tf_op jit(solution)/shard_map/ppermute | solution.py:294
  106.0 0.0 collective-permute-done.11
  106.0 0.9 collective-permute-done.10
  106.9 0.1 collective-permute-start.15
  107.0 0.1 collective-permute-start.14
  107.1 4.0 %collective-permute-start.13 = (f32[128,128]{1,0:T(8,128)S(1)}, f32[128,128]{1,0:T(8,128)S(1)}, u32[]{:S(2)}, u32[]{:S(2)}) collective-permute-start(f32[128,128]{1,0:T(8,128)S(1)} %add_add_fusion.2), channel_id=1, source_target_pairs={{0,4},{1,5},{2,6},{3,7},{4,0},{5,1},{6,2},{7,3},{8,12},{9,13},{10,... | collective-permute-start | bytes 196616 | tf_op jit(solution)/shard_map/ppermute | solution.py:294
  111.1 2.1 %collective-permute-done.15 = f32[128,128]{1,0:T(8,128)S(1)} collective-permute-done((f32[128,128]{1,0:T(8,128)S(1)}, f32[128,128]{1,0:T(8,128)S(1)}, u32[]{:S(2)}, u32[]{:S(2)}) %collective-permute-start.15) | collective-permute-done | bytes 65568 | tf_op jit(solution)/shard_map/ppermute | solution.py:294
  113.2 0.0 collective-permute-done.14
  113.2 0.9 collective-permute-done.13
  114.1 0.1 collective-permute-start.16
  114.1 1.2 collective-permute-done.16
  115.4 3.8 %collective-permute-start.19 = (f32[128,128]{1,0:T(8,128)S(1)}, f32[128,128]{1,0:T(8,128)S(1)}, u32[]{:S(2)}, u32[]{:S(2)}) collective-permute-start(f32[128,128]{1,0:T(8,128)S(1)} %add.36), channel_id=1, source_target_pairs={{0,96},{1,97},{2,98},{3,99},{4,100},{5,101},{6,102},{7,103},{8,104... | collective-permute-start | bytes 196616 | tf_op jit(solution)/shard_map/ppermute | solution.py:294
  119.2 0.0 collective-permute-start.18
  119.2 0.9 collective-permute-start.17
  120.1 2.2 %collective-permute-done.19 = f32[128,128]{1,0:T(8,128)S(1)} collective-permute-done((f32[128,128]{1,0:T(8,128)S(1)}, f32[128,128]{1,0:T(8,128)S(1)}, u32[]{:S(2)}, u32[]{:S(2)}) %collective-permute-start.19) | collective-permute-done | bytes 65568 | tf_op jit(solution)/shard_map/ppermute | solution.py:294
  122.3 3.0 %collective-permute-done.18 = f32[128,128]{1,0:T(8,128)S(1)} collective-permute-done((f32[128,128]{1,0:T(8,128)S(1)}, f32[128,128]{1,0:T(8,128)S(1)}, u32[]{:S(2)}, u32[]{:S(2)}) %collective-permute-start.18) | collective-permute-done | bytes 65568 | tf_op jit(solution)/shard_map/ppermute | solution.py:294
  125.2 0.0 collective-permute-done.17
  125.3 4.3 %shard_map.75 = f32[1024,128]{1,0:T(8,128)} custom-call(f32[128,128]{1,0:T(8,128)S(1)} %add_add_fusion.gram, bf16[1024,128]{1,0:T(8,128)(2,1)S(1)} %get-tuple-element.52.y), custom_call_target="tpu_custom_call" | custom-call | flops 536870912 | bytes 1000000 | tf_op jit(solution)/shard_map/pallas_call | solution.py:359
  (11 shorter events, 0.1 us)
Async XLA Ops:
  0.0 2.5 %copy-start = (bf16[4,10,256,256]{3,2,1,0:T(8,128)(2,1)S(1)}, bf16[4,10,256,256]{3,2,1,0:T(8,128)(2,1)}, u32[]{:S(2)}) copy-start(bf16[4,10,256,256]{3,2,1,0:T(8,128)(2,1)} %blocks.1) | copy-start | bytes 15728644
  2.5 0.9 copy-start.1
  3.4 0.7 copy-start.5
  4.1 0.7 copy-start.6
  4.8 0.7 copy-start.7
  5.5 14.1 %copy-start.8 = (f32[1024]{0:T(1024)S(1)}, f32[1024]{0:T(1024)}, u32[]{:S(2)}) copy-start(f32[1024]{0:T(1024)} %param.10) | copy-start | bytes 12292
  5.5 14.4 %copy-start.2 = (bf16[1024,128]{1,0:T(8,128)(2,1)S(1)}, bf16[1024,128]{1,0:T(8,128)(2,1)}, u32[]{:S(2)}) copy-start(bf16[1024,128]{1,0:T(8,128)(2,1)} %older.1) | copy-start | bytes 786436
  10.1 1.3 %copy-start.3 = (bf16[1024,1024]{1,0:T(8,128)(2,1)}, bf16[1024,1024]{1,0:T(8,128)(2,1)S(1)}, u32[]{:S(2)}) copy-start(bf16[1024,1024]{1,0:T(8,128)(2,1)S(1)} %get-tuple-element.29.own) | copy-start | bytes 6291460
  11.4 26.0 %collective-permute-start = (bf16[3072,128]{1,0:T(8,128)(2,1)}, bf16[3072,128]{1,0:T(8,128)(2,1)}, u32[]{:S(2)}, u32[]{:S(2)}) collective-permute-start(bf16[3072,128]{1,0:T(8,128)(2,1)} %get-tuple-element.35.to_right), channel_id=1, source_target_pairs={{0,1},{1,2},{2,3},{3,4},{4,5},{5,6},{6,7},{7,8},{8,9},{9,10},{10,1... | collective-permute-start | bytes 2359304 | tf_op jit(solution)/shard_map/ppermute | solution.py:282
  13.2 24.3 %collective-permute-start.1 = (bf16[3072,128]{1,0:T(8,128)(2,1)}, bf16[3072,128]{1,0:T(8,128)(2,1)}, u32[]{:S(2)}, u32[]{:S(2)}) collective-permute-start(bf16[3072,128]{1,0:T(8,128)(2,1)} %get-tuple-element.36.to_left), channel_id=1, source_target_pairs={{0,127},{1,0},{2,1},{3,2},{4,3},{5,4},{6,5},{7,6},{8,7},{9,8},{10,... | collective-permute-start | bytes 2359304 | tf_op jit(solution)/shard_map/ppermute | solution.py:282
  19.8 1.6 %copy-start.4 = (bf16[1024,1024]{1,0:T(8,128)(2,1)S(1)}, bf16[1024,1024]{1,0:T(8,128)(2,1)}, u32[]{:S(2)}) copy-start(bf16[1024,1024]{1,0:T(8,128)(2,1)} %copy-done.3) | copy-start | bytes 6291460
  41.6 13.6 %collective-permute-start.2 = (bf16[1024,128]{1,0:T(8,128)(2,1)S(1)}, bf16[1024,128]{1,0:T(8,128)(2,1)S(1)}, u32[]{:S(2)}, u32[]{:S(2)}) collective-permute-start(bf16[1024,128]{1,0:T(8,128)(2,1)S(1)} %get-tuple-element.40), channel_id=1, source_target_pairs={{0,1},{1,2},{2,3},{3,4},{4,5},{5,6},{6,7},{7,8},{8,9},{9,10},{10,1... | collective-permute-start | bytes 786440 | tf_op jit(solution)/shard_map/ppermute | solution.py:282
  41.7 13.5 %collective-permute-start.3 = (bf16[1024,128]{1,0:T(8,128)(2,1)S(1)}, bf16[1024,128]{1,0:T(8,128)(2,1)S(1)}, u32[]{:S(2)}, u32[]{:S(2)}) collective-permute-start(bf16[1024,128]{1,0:T(8,128)(2,1)S(1)} %get-tuple-element.41), channel_id=1, source_target_pairs={{0,127},{1,0},{2,1},{3,2},{4,3},{5,4},{6,5},{7,6},{8,7},{9,8},{10,... | collective-permute-start | bytes 786440 | tf_op jit(solution)/shard_map/ppermute | solution.py:282
  56.4 13.8 %collective-permute-start.4 = (bf16[1024,128]{1,0:T(8,128)(2,1)S(1)}, bf16[1024,128]{1,0:T(8,128)(2,1)S(1)}, u32[]{:S(2)}, u32[]{:S(2)}) collective-permute-start(bf16[1024,128]{1,0:T(8,128)(2,1)S(1)} %get-tuple-element.43), channel_id=1, source_target_pairs={{0,1},{1,2},{2,3},{3,4},{4,5},{5,6},{6,7},{7,8},{8,9},{9,10},{10,1... | collective-permute-start | bytes 786440 | tf_op jit(solution)/shard_map/ppermute | solution.py:282
  56.5 13.7 %collective-permute-start.5 = (bf16[1024,128]{1,0:T(8,128)(2,1)S(1)}, bf16[1024,128]{1,0:T(8,128)(2,1)S(1)}, u32[]{:S(2)}, u32[]{:S(2)}) collective-permute-start(bf16[1024,128]{1,0:T(8,128)(2,1)S(1)} %get-tuple-element.44), channel_id=1, source_target_pairs={{0,127},{1,0},{2,1},{3,2},{4,3},{5,4},{6,5},{7,6},{8,7},{9,8},{10,... | collective-permute-start | bytes 786440 | tf_op jit(solution)/shard_map/ppermute | solution.py:282
  71.5 13.7 %collective-permute-start.6 = (bf16[1024,128]{1,0:T(8,128)(2,1)S(1)}, bf16[1024,128]{1,0:T(8,128)(2,1)S(1)}, u32[]{:S(2)}, u32[]{:S(2)}) collective-permute-start(bf16[1024,128]{1,0:T(8,128)(2,1)S(1)} %get-tuple-element.46), channel_id=1, source_target_pairs={{0,1},{1,2},{2,3},{3,4},{4,5},{5,6},{6,7},{7,8},{8,9},{9,10},{10,1... | collective-permute-start | bytes 786440 | tf_op jit(solution)/shard_map/ppermute | solution.py:282
  71.6 13.6 %collective-permute-start.7 = (bf16[1024,128]{1,0:T(8,128)(2,1)S(1)}, bf16[1024,128]{1,0:T(8,128)(2,1)S(1)}, u32[]{:S(2)}, u32[]{:S(2)}) collective-permute-start(bf16[1024,128]{1,0:T(8,128)(2,1)S(1)} %get-tuple-element.47), channel_id=1, source_target_pairs={{0,127},{1,0},{2,1},{3,2},{4,3},{5,4},{6,5},{7,6},{8,7},{9,8},{10,... | collective-permute-start | bytes 786440 | tf_op jit(solution)/shard_map/ppermute | solution.py:282
  86.5 12.3 %collective-permute-start.8 = (bf16[1024,128]{1,0:T(8,128)(2,1)S(1)}, bf16[1024,128]{1,0:T(8,128)(2,1)S(1)}, u32[]{:S(2)}, u32[]{:S(2)}) collective-permute-start(bf16[1024,128]{1,0:T(8,128)(2,1)S(1)} %get-tuple-element.49), channel_id=1, source_target_pairs={{0,1},{1,2},{2,3},{3,4},{4,5},{5,6},{6,7},{7,8},{8,9},{9,10},{10,1... | collective-permute-start | bytes 786440 | tf_op jit(solution)/shard_map/ppermute | solution.py:282
  86.6 12.3 %collective-permute-start.9 = (bf16[1024,128]{1,0:T(8,128)(2,1)S(1)}, bf16[1024,128]{1,0:T(8,128)(2,1)S(1)}, u32[]{:S(2)}, u32[]{:S(2)}) collective-permute-start(bf16[1024,128]{1,0:T(8,128)(2,1)S(1)} %get-tuple-element.50), channel_id=1, source_target_pairs={{0,127},{1,0},{2,1},{3,2},{4,3},{5,4},{6,5},{7,6},{8,7},{9,8},{10,... | collective-permute-start | bytes 786440 | tf_op jit(solution)/shard_map/ppermute | solution.py:282
  99.8 6.3 %collective-permute-start.12 = (f32[128,128]{1,0:T(8,128)S(1)}, f32[128,128]{1,0:T(8,128)S(1)}, u32[]{:S(2)}, u32[]{:S(2)}) collective-permute-start(f32[128,128]{1,0:T(8,128)S(1)} %get-tuple-element.51), channel_id=1, source_target_pairs={{0,3},{1,2},{2,1},{3,0},{4,7},{5,6},{6,5},{7,4},{8,11},{9,10},{10,... | collective-permute-start | bytes 196616 | tf_op jit(solution)/shard_map/ppermute | solution.py:294
  99.9 6.2 %collective-permute-start.11 = (f32[128,128]{1,0:T(8,128)S(1)}, f32[128,128]{1,0:T(8,128)S(1)}, u32[]{:S(2)}, u32[]{:S(2)}) collective-permute-start(f32[128,128]{1,0:T(8,128)S(1)} %get-tuple-element.51), channel_id=1, source_target_pairs={{0,2},{1,3},{2,0},{3,1},{4,6},{5,7},{6,4},{7,5},{8,10},{9,11},{10,... | collective-permute-start | bytes 196616 | tf_op jit(solution)/shard_map/ppermute | solution.py:294
  100.0 6.9 %collective-permute-start.10 = (f32[128,128]{1,0:T(8,128)S(1)}, f32[128,128]{1,0:T(8,128)S(1)}, u32[]{:S(2)}, u32[]{:S(2)}) collective-permute-start(f32[128,128]{1,0:T(8,128)S(1)} %get-tuple-element.51), channel_id=1, source_target_pairs={{0,1},{1,0},{2,3},{3,2},{4,5},{5,4},{6,7},{7,6},{8,9},{9,8},{10,11... | collective-permute-start | bytes 196616 | tf_op jit(solution)/shard_map/ppermute | solution.py:294
  106.9 6.3 %collective-permute-start.15 = (f32[128,128]{1,0:T(8,128)S(1)}, f32[128,128]{1,0:T(8,128)S(1)}, u32[]{:S(2)}, u32[]{:S(2)}) collective-permute-start(f32[128,128]{1,0:T(8,128)S(1)} %add_add_fusion.2), channel_id=1, source_target_pairs={{0,12},{1,13},{2,14},{3,15},{4,8},{5,9},{6,10},{7,11},{8,4},{9,5},... | collective-permute-start | bytes 196616 | tf_op jit(solution)/shard_map/ppermute | solution.py:294
  107.0 6.2 %collective-permute-start.14 = (f32[128,128]{1,0:T(8,128)S(1)}, f32[128,128]{1,0:T(8,128)S(1)}, u32[]{:S(2)}, u32[]{:S(2)}) collective-permute-start(f32[128,128]{1,0:T(8,128)S(1)} %add_add_fusion.2), channel_id=1, source_target_pairs={{0,8},{1,9},{2,10},{3,11},{4,12},{5,13},{6,14},{7,15},{8,0},{9,1},... | collective-permute-start | bytes 196616 | tf_op jit(solution)/shard_map/ppermute | solution.py:294
  107.1 6.9 %collective-permute-start.13 = (f32[128,128]{1,0:T(8,128)S(1)}, f32[128,128]{1,0:T(8,128)S(1)}, u32[]{:S(2)}, u32[]{:S(2)}) collective-permute-start(f32[128,128]{1,0:T(8,128)S(1)} %add_add_fusion.2), channel_id=1, source_target_pairs={{0,4},{1,5},{2,6},{3,7},{4,0},{5,1},{6,2},{7,3},{8,12},{9,13},{10,... | collective-permute-start | bytes 196616 | tf_op jit(solution)/shard_map/ppermute | solution.py:294
  114.1 1.3 %collective-permute-start.16 = (f32[128,128]{1,0:T(8,128)S(1)}, f32[128,128]{1,0:T(8,128)S(1)}, u32[]{:S(2)}, u32[]{:S(2)}) collective-permute-start(f32[128,128]{1,0:T(8,128)S(1)} %add_add_fusion.1), channel_id=1, source_target_pairs={{0,16},{1,17},{2,18},{3,19},{4,20},{5,21},{6,22},{7,23},{8,24},{9,... | collective-permute-start | bytes 196616 | tf_op jit(solution)/shard_map/ppermute | solution.py:294
  115.4 6.9 %collective-permute-start.19 = (f32[128,128]{1,0:T(8,128)S(1)}, f32[128,128]{1,0:T(8,128)S(1)}, u32[]{:S(2)}, u32[]{:S(2)}) collective-permute-start(f32[128,128]{1,0:T(8,128)S(1)} %add.36), channel_id=1, source_target_pairs={{0,96},{1,97},{2,98},{3,99},{4,100},{5,101},{6,102},{7,103},{8,104... | collective-permute-start | bytes 196616 | tf_op jit(solution)/shard_map/ppermute | solution.py:294
  119.2 6.1 %collective-permute-start.18 = (f32[128,128]{1,0:T(8,128)S(1)}, f32[128,128]{1,0:T(8,128)S(1)}, u32[]{:S(2)}, u32[]{:S(2)}) collective-permute-start(f32[128,128]{1,0:T(8,128)S(1)} %add.36), channel_id=1, source_target_pairs={{0,64},{1,65},{2,66},{3,67},{4,68},{5,69},{6,70},{7,71},{8,72},{9,... | collective-permute-start | bytes 196616 | tf_op jit(solution)/shard_map/ppermute | solution.py:294
  119.2 6.1 %collective-permute-start.17 = (f32[128,128]{1,0:T(8,128)S(1)}, f32[128,128]{1,0:T(8,128)S(1)}, u32[]{:S(2)}, u32[]{:S(2)}) collective-permute-start(f32[128,128]{1,0:T(8,128)S(1)} %add.36), channel_id=1, source_target_pairs={{0,32},{1,33},{2,34},{3,35},{4,36},{5,37},{6,38},{7,39},{8,40},{9,... | collective-permute-start | bytes 196616 | tf_op jit(solution)/shard_map/ppermute | solution.py:294
